TPU v7x, 256 devices: a whole 4x4x8 slice. The times are simulated.
256 devices in a mesh: prow: 16 (over z, core), pcol: 16 (over x, y).
Axes of the slice: x: 4, y: 4, z: 8, core: 2. Of those that a mesh axis runs over, the one named last changes fastest.
Arguments:
- leaf_source: bfloat16 [16, 16, 8, 256, 128], P('prow', 'pcol'), may hold values from -6 to 6
- band_source: bfloat16 [16, 256, 128], P('prow'), may hold values from -6 to 6
- strip_source: bfloat16 [16, 256, 128], P('pcol'), may hold values from -6 to 6
- summit_source: bfloat16 [256, 128], replicated, may hold values from -6 to 6
- leaf_inverse: bfloat16 [16, 16, 8, 256, 256], P('prow', 'pcol'), may hold values from -1 to 2
- band_inverse: bfloat16 [16, 256, 256], P('prow'), may hold values from -1 to 2
- strip_inverse: bfloat16 [16, 256, 256], P('pcol'), may hold values from -1 to 2
- summit_inverse: bfloat16 [256, 256], replicated, may hold values from -1 to 2
- leaf_blocks: bfloat16 [16, 16, 28, 256, 256], P('prow', 'pcol'), may hold values from -0.09375 to 0.09375
- band_blocks: bfloat16 [16, 16, 8, 256, 256], P('prow', 'pcol'), may hold values from -0.0234375 to 0.0234375
- strip_blocks: bfloat16 [16, 16, 8, 256, 256], P('prow', 'pcol'), may hold values from -0.0234375 to 0.0234375
- summit_blocks: bfloat16 [16, 16, 8, 256, 256], P('prow', 'pcol'), may hold values from -0.015625 to 0.015625
- coupling: bfloat16 [16, 16, 256, 256], P('prow', 'pcol'), may hold values from -0.0625 to 0.0625
- summit_band: bfloat16 [16, 256, 256], P('prow', 'pcol'), may hold values from -0.046875 to 0.046875
- summit_strip: bfloat16 [16, 256, 256], P('pcol'), may hold values from -0.046875 to 0.046875
- parents: int32 [16, 16, 8], P('prow', 'pcol'), may hold values from 1 to 8, as said below
- widths: int32 [16, 16, 8], P('prow', 'pcol'), may hold values from 64 to 256
Outputs:
- leaf_answer: bfloat16 [16, 16, 8, 256, 128], P('prow', 'pcol')
- band_answer: bfloat16 [16, 256, 128], P('prow')
- strip_answer: bfloat16 [16, 256, 128], P('pcol')
- summit_answer: bfloat16 [256, 128], replicated
Inputs may be any that keep to these rules, and one draw needn't show every extreme that they name: parents[r, c, a] is a later leaf of the same subtree, or 8 where leaf a links only to the separators.
All inputs are finite; a program needn't handle non-finite values.
Results may differ from a plain program's by a relative error of at most 0.015.
Values sent between devices are 32-bit elements; how exact they have to be, the bound alone decides.
A program may use at most 64 MiB of HBM per device.

v0:
```python
import jax
import jax.numpy as jnp
from jax import lax
from jax.sharding import PartitionSpec as P

PASSES = 2


def ancestors(parent_list, leaf_count):
    node_ids = jnp.arange(leaf_count + 1, dtype=jnp.int32)
    current = parent_list
    extended = jnp.concatenate([current, jnp.full((1,), leaf_count, jnp.int32)])
    reached = jnp.zeros((leaf_count + 1, leaf_count), jnp.float32)
    for repeat in range(leaf_count):
        matches = current[None, :] == node_ids[:, None]
        reached = jnp.maximum(reached, matches.astype(jnp.float32))
        current = jnp.sum(jnp.where(matches, extended[:, None], 0), axis=0)
    return reached[:leaf_count]


def multiply(left, right, form):
    return jnp.einsum(form, left, right, preferred_element_type=jnp.float32)


def forward_block(inverse, source, partial_value):
    residual = (source.astype(jnp.float32) - partial_value).astype(jnp.bfloat16)
    return multiply(inverse, residual, "ij,jr->ir").astype(jnp.bfloat16)


def backward_block(inverse, source, partial_value):
    residual = (source.astype(jnp.float32) - partial_value).astype(jnp.bfloat16)
    return multiply(inverse, residual, "ji,jr->ir").astype(jnp.bfloat16)


def leaf_forward(pair_blocks, inverses, sources, reached, row_mask):
    leaf_count = sources.shape[0]
    solved = []
    for position in range(leaf_count):
        residual = sources[position].astype(jnp.float32)
        if position > 0:
            first_pair = position * (position - 1) // 2
            weights = reached[position, :position].astype(jnp.bfloat16)
            stacked = jnp.stack(solved) * weights[:, None, None]
            residual = residual - multiply(
                pair_blocks[first_pair : first_pair + position], stacked, "bij,bjr->ir"
            )
        residual = (row_mask[position] * residual).astype(jnp.bfloat16)
        solved.append(
            (row_mask[position] * multiply(inverses[position], residual, "ij,jr->ir")).astype(
                jnp.bfloat16
            )
        )
    return jnp.stack(solved)


def leaf_backward(pair_blocks, inverses, solved, outer, reached, row_mask):
    leaf_count = solved.shape[0]
    pending = outer
    answers = [None] * leaf_count
    for position in reversed(range(leaf_count)):
        residual = (
            row_mask[position] * (solved[position].astype(jnp.float32) - pending[position])
        ).astype(jnp.bfloat16)
        update = (row_mask[position] * multiply(inverses[position], residual, "ji,jr->ir")).astype(
            jnp.bfloat16
        )
        answers[position] = update
        if position > 0:
            first_pair = position * (position - 1) // 2
            pushed = multiply(
                pair_blocks[first_pair : first_pair + position], update, "bji,jr->bir"
            )
            pending = pending.at[:position].add(
                reached[position, :position][:, None, None] * pushed
            )
    return jnp.stack(answers)


def per_device(
    leaf_source,
    band_source,
    strip_source,
    summit_source,
    leaf_inverse,
    band_inverse,
    strip_inverse,
    summit_inverse,
    leaf_blocks,
    band_blocks,
    strip_blocks,
    summit_blocks,
    coupling,
    summit_band,
    summit_strip,
    parents,
    widths,
):
    leaf_count = leaf_source.shape[2]
    block_width = leaf_source.shape[3]
    reached = ancestors(parents[0, 0], leaf_count)
    column_ids = jnp.arange(block_width, dtype=jnp.int32)
    row_mask = (column_ids[None, :] < widths[0, 0][:, None]).astype(jnp.float32)[:, :, None]
    band_slab = summit_band.shape[1]
    strip_slab = block_width // lax.axis_size("prow")
    column_place = lax.axis_index("pcol") * band_slab
    row_place = lax.axis_index("prow") * strip_slab
    inverses = leaf_inverse[0, 0]
    pair_blocks = leaf_blocks[0, 0]
    to_band = band_blocks[0, 0]
    to_strip = strip_blocks[0, 0]
    to_summit = summit_blocks[0, 0]
    link_block = coupling[0, 0]
    lift_band = summit_band[0]
    lift_strip = summit_strip[0]
    current = (leaf_source[0, 0], band_source[0], strip_source[0], summit_source)
    for iteration in range(PASSES):
        leaf_now, band_now, strip_now, summit_now = current
        solved = leaf_forward(pair_blocks, inverses, leaf_now, reached, row_mask)
        band_term = multiply(to_band, solved, "aij,ajr->ir")
        strip_term = multiply(to_strip, solved, "aij,ajr->ir")
        summit_term = multiply(to_summit, solved, "aij,ajr->ir")
        band_partial = lax.psum(band_term, "pcol")
        band_solved = forward_block(band_inverse[0], band_now, band_partial)
        own_band = lax.dynamic_slice_in_dim(band_solved, column_place, band_slab, 0)
        summit_term = summit_term + multiply(lift_band, own_band, "ki,kn->in")
        strip_term = strip_term + multiply(link_block, band_solved, "ij,jn->in")
        strip_partial = lax.psum(strip_term, "prow")
        strip_solved = forward_block(strip_inverse[0], strip_now, strip_partial)
        own_lift = lax.dynamic_slice_in_dim(lift_strip, row_place, strip_slab, 0)
        own_strip = lax.dynamic_slice_in_dim(strip_solved, row_place, strip_slab, 0)
        summit_partial = lax.psum(
            summit_term + multiply(own_lift, own_strip, "ki,kn->in"), ("prow", "pcol")
        )
        summit_solved = forward_block(summit_inverse, summit_now, summit_partial)
        summit_answer = backward_block(
            summit_inverse, summit_solved, jnp.zeros(summit_solved.shape, jnp.float32)
        )
        strip_answer = backward_block(
            strip_inverse[0], strip_solved, multiply(lift_strip, summit_answer, "ki,in->kn")
        )
        downward = multiply(link_block, strip_answer, "ji,jn->in")
        band_piece = multiply(lift_band, summit_answer, "ki,in->kn")
        band_back = lax.psum(downward, "pcol") + lax.all_gather(
            band_piece, "pcol", axis=0, tiled=True
        )
        band_answer = backward_block(band_inverse[0], band_solved, band_back)
        outer = (
            multiply(to_band, band_answer, "aij,ir->ajr")
            + multiply(to_strip, strip_answer, "aij,ir->ajr")
            + multiply(to_summit, summit_answer, "aij,ir->ajr")
        )
        leaf_answer = leaf_backward(pair_blocks, inverses, solved, outer, reached, row_mask)
        current = (leaf_answer, band_answer, strip_answer, summit_answer)
    return (current[0][None, None], current[1][None], current[2][None], current[3])


def solution(mesh):
    placed = (
        P("prow", "pcol", None, None, None),
        P("prow", None, None),
        P("pcol", None, None),
        P(),
        P("prow", "pcol", None, None, None),
        P("prow", None, None),
        P("pcol", None, None),
        P(),
        P("prow", "pcol", None, None, None),
        P("prow", "pcol", None, None, None),
        P("prow", "pcol", None, None, None),
        P("prow", "pcol", None, None, None),
        P("prow", "pcol", None, None),
        P("prow", "pcol", None),
        P("pcol", None, None),
        P("prow", "pcol", None),
        P("prow", "pcol", None),
    )
    return jax.shard_map(
        per_device,
        mesh=mesh,
        in_specs=placed,
        out_specs=(
            P("prow", "pcol", None, None, None),
            P("prow", None, None),
            P("pcol", None, None),
            P(),
        ),
        check_vma=False,
    )
```

profile of v0, /device:TPU:1, one launch (start us, length us, event | category | flops | bytes accessed | tf_op | source)
XLA Modules:
  0.0 1181.4 jit_solution(3843605746356094015)
XLA Ops:
  12.2 1.1 fusion.591
  14.1 1.9 constant_dynamic-update-slice_fusion.17
  15.9 2.0 constant_dynamic-update-slice_fusion.16
  17.9 2.1 constant_dynamic-update-slice_fusion.15
  20.0 2.1 constant_dynamic-update-slice_fusion.14
  22.1 2.2 constant_dynamic-update-slice_fusion.13
  25.3 2.5 constant_dynamic-update-slice_fusion.12
  28.6 2.6 constant_dynamic-update-slice_fusion.11
  31.2 2.6 constant_dynamic-update-slice_fusion.18
  33.8 2.2 convolution_bitcast_fusion.19
  36.1 1.3 slice_bitcast_fusion.14
  37.3 1.3 slice_bitcast_fusion.15
  38.6 1.2 slice_bitcast_fusion.16
  39.8 1.3 slice_bitcast_fusion.17
  41.0 1.3 slice_bitcast_fusion.18
  42.3 2.1 convolution_bitcast_fusion.17
  44.4 2.1 convolution_bitcast_fusion.18
  46.5 84.2 %all-reduce.9.cloned.1.call-done = f32[256,128]{1,0:T(8,128)} async-done(((f32[256,128]{1,0:T(8,128)}), f32[256,128]{1,0:T(8,128)}) %all-reduce.9.cloned.1.call-update) | async-done | bytes 131088 | tf_op jit(solution)/shard_map/psum | solution.py:122
  130.8 1.2 convolution_convert_fusion.11
  132.6 1.7 fusion.29
  134.4 1.8 fusion.34
  136.3 106.7 %all-reduce.11.cloned.1.call-done = f32[256,128]{1,0:T(8,128)} async-done(((f32[256,128]{1,0:T(8,128)}), f32[256,128]{1,0:T(8,128)}) %all-reduce.11.cloned.1.call-update) | async-done | bytes 131088 | tf_op jit(solution)/shard_map/psum | solution.py:127
  243.0 1.1 convolution_convert_fusion.10
  244.7 1.8 convolution_add_fusion.8
  246.6 1.2 slice_bitcast_fusion.19
  247.8 242.5 %all-reduce.13.cloned.1.call-done = f32[256,128]{1,0:T(8,128)} async-done(((f32[256,128]{1,0:T(8,128)}), f32[256,128]{1,0:T(8,128)}) %all-reduce.13.cloned.1.call-update) | async-done | bytes 131088 | tf_op jit(solution)/shard_map/psum | solution.py:131
  490.3 1.9 convolution_convert_fusion.8
  492.1 1.9 convolution_convert_fusion.7
  494.0 1.7 convolution_bitcast_fusion.10
  496.7 19.7 %all_gather.6 = f32[256,128]{1,0:T(8,128)} all-gather(f32[16,128]{1,0:T(8,128)S(1)} %convolution_bitcast_fusion.22), channel_id=1, replica_groups=mesh['prow'=16,'pcol'=16] {'pcol'}, dimensions={0}, use_global_device_ids=true | all-gather | bytes 139264 | tf_op jit(solution)/shard_map/all_gather | solution.py:143
  516.4 1.6 copy.39
  518.1 66.1 %all-reduce.15.cloned.1.call-done = f32[256,128]{0,1:T(8,128)} async-done(((f32[256,128]{0,1:T(8,128)}), f32[256,128]{0,1:T(8,128)}) %all-reduce.15.cloned.1.call-update) | async-done | bytes 131088 | tf_op jit(solution)/shard_map/psum | solution.py:143
  584.2 1.2 convolution_convert_fusion.6
  586.5 1.3 convolution_add_fusion.3
  593.0 1.5 fusion.77
  594.5 2.0 constant_dynamic-update-slice_fusion.43
  596.5 2.1 constant_dynamic-update-slice_fusion.42
  598.6 2.2 constant_dynamic-update-slice_fusion.41
  600.8 2.4 constant_dynamic-update-slice_fusion.40
  603.2 2.4 constant_dynamic-update-slice_fusion.39
  605.6 2.5 constant_dynamic-update-slice_fusion.38
  608.1 2.6 constant_dynamic-update-slice_fusion.37
  610.7 2.7 constant_dynamic-update-slice_fusion.44
  613.4 2.2 convolution_bitcast_fusion.13
  615.6 2.2 convolution_bitcast_fusion.15
  617.8 2.2 convolution_bitcast_fusion.14
  620.0 89.7 %all-reduce.17.cloned.1.call-done = f32[256,128]{0,1:T(8,128)} async-done(((f32[256,128]{0,1:T(8,128)}), f32[256,128]{0,1:T(8,128)}) %all-reduce.17.cloned.1.call-update) | async-done | bytes 131088 | tf_op jit(solution)/shard_map/psum | solution.py:122
  709.7 1.2 convolution_convert_fusion.5
  711.6 1.8 fusion.27
  713.4 1.8 fusion.33
  715.2 106.8 %all-reduce.19.cloned.1.call-done = f32[256,128]{0,1:T(8,128)} async-done(((f32[256,128]{0,1:T(8,128)}), f32[256,128]{0,1:T(8,128)}) %all-reduce.19.cloned.1.call-update) | async-done | bytes 131088 | tf_op jit(solution)/shard_map/psum | solution.py:127
  822.0 1.1 convolution_convert_fusion.4
  823.7 1.8 convolution_add_fusion.6
  825.6 244.6 %all-reduce.21.cloned.1.call-done = f32[256,128]{0,1:T(8,128)} async-done(((f32[256,128]{0,1:T(8,128)}), f32[256,128]{0,1:T(8,128)}) %all-reduce.21.cloned.1.call-update) | async-done | bytes 131088 | tf_op jit(solution)/shard_map/psum | solution.py:131
  1070.2 1.9 convolution_convert_fusion.2
  1072.1 1.3 convolution_convert_fusion.1
  1075.2 1.6 copy.44
  1077.5 18.4 %all_gather.7 = f32[256,128]{1,0:T(8,128)S(1)} all-gather(f32[16,128]{1,0:T(8,128)S(1)} %convolution_bitcast_fusion.21), channel_id=1, replica_groups=mesh['prow'=16,'pcol'=16] {'pcol'}, dimensions={0}, use_global_device_ids=true | all-gather | bytes 139264 | tf_op jit(solution)/shard_map/all_gather | solution.py:143
  1096.7 66.1 %all-reduce.23.cloned.1.call-done = f32[256,128]{0,1:T(8,128)} async-done(((f32[256,128]{0,1:T(8,128)}), f32[256,128]{0,1:T(8,128)}) %all-reduce.23.cloned.1.call-update) | async-done | bytes 131088 | tf_op jit(solution)/shard_map/psum | solution.py:143
  1162.8 1.2 convolution_convert_fusion
  1164.0 1.3 fusion.130
  1166.1 1.7 convolution_add_fusion.1
  1171.5 2.0 fusion.121
  1173.6 1.0 copy.41
  (253 shorter events, 23.8 us)
Async XLA Ops:
  7.2 26.6 %copy-start = (bf16[1,1,8,256,256]{4,3,2,1,0:T(8,128)(2,1)S(1)}, bf16[1,1,8,256,256]{4,3,2,1,0:T(8,128)(2,1)}, u32[]{:S(2)}) copy-start(bf16[1,1,8,256,256]{4,3,2,1,0:T(8,128)(2,1)} %param.54) | copy-start | bytes 3145732
  7.2 123.6 %all-reduce.9.cloned.1.call-start = ((), (), s32[]{:S(2)}) async-start(), calls=%async_computation | async-start | bytes 262144 | tf_op jit(solution)/shard_map/psum | solution.py:122
  10.6 20.6 %copy-start.79 = (bf16[7]{0:T(256)(128)(2,1)}, bf16[7]{0:T(256)(128)(2,1)S(1)}, u32[]{:S(2)}) copy-start(bf16[7]{0:T(256)(128)(2,1)S(1)} %fusion.590) | copy-start | bytes 46
  10.6 18.0 %copy-start.80 = (bf16[6]{0:T(256)(128)(2,1)}, bf16[6]{0:T(256)(128)(2,1)S(1)}, u32[]{:S(2)}) copy-start(bf16[6]{0:T(256)(128)(2,1)S(1)} %fusion.589) | copy-start | bytes 40
  10.6 14.7 %copy-start.81 = (bf16[5]{0:T(256)(128)(2,1)}, bf16[5]{0:T(256)(128)(2,1)S(1)}, u32[]{:S(2)}) copy-start(bf16[5]{0:T(256)(128)(2,1)S(1)} %fusion.588) | copy-start | bytes 34
  10.7 13.6 %copy-start.82 = (bf16[4]{0:T(256)(128)(2,1)}, bf16[4]{0:T(256)(128)(2,1)S(1)}, u32[]{:S(2)}) copy-start(bf16[4]{0:T(256)(128)(2,1)S(1)} %fusion.587) | copy-start | bytes 28
  10.7 13.6 %copy-start.83 = (bf16[3]{0:T(256)(128)(2,1)}, bf16[3]{0:T(256)(128)(2,1)S(1)}, u32[]{:S(2)}) copy-start(bf16[3]{0:T(256)(128)(2,1)S(1)} %fusion.586) | copy-start | bytes 22
  10.7 13.6 %copy-start.84 = (bf16[2]{0:T(256)(128)(2,1)}, bf16[2]{0:T(256)(128)(2,1)S(1)}, u32[]{:S(2)}) copy-start(bf16[2]{0:T(256)(128)(2,1)S(1)} %fusion.585) | copy-start | bytes 16
  12.1 12.2 %copy-start.45 = (f32[1,256]{1,0:T(1,128)}, f32[1,256]{1,0:T(1,128)S(1)}, u32[]{:S(2)}) copy-start(f32[1,256]{1,0:T(1,128)S(1)} %get-tuple-element.241) | copy-start | bytes 3076
  12.2 12.2 %copy-start.48 = (f32[1,256]{1,0:T(1,128)}, f32[1,256]{1,0:T(1,128)S(1)}, u32[]{:S(2)}) copy-start(f32[1,256]{1,0:T(1,128)S(1)} %get-tuple-element.240) | copy-start | bytes 3076
  12.2 12.2 %copy-start.61 = (f32[1,256]{1,0:T(1,128)}, f32[1,256]{1,0:T(1,128)S(1)}, u32[]{:S(2)}) copy-start(f32[1,256]{1,0:T(1,128)S(1)} %get-tuple-element.244) | copy-start | bytes 3076
  12.2 13.1 %copy-start.51 = (f32[1,256]{1,0:T(1,128)}, f32[1,256]{1,0:T(1,128)S(1)}, u32[]{:S(2)}) copy-start(f32[1,256]{1,0:T(1,128)S(1)} %get-tuple-element.239) | copy-start | bytes 3076
  12.2 16.4 %copy-start.54 = (f32[1,256]{1,0:T(1,128)}, f32[1,256]{1,0:T(1,128)S(1)}, u32[]{:S(2)}) copy-start(f32[1,256]{1,0:T(1,128)S(1)} %get-tuple-element.238) | copy-start | bytes 3076
  12.2 19.0 %copy-start.57 = (f32[1,256]{1,0:T(1,128)}, f32[1,256]{1,0:T(1,128)S(1)}, u32[]{:S(2)}) copy-start(f32[1,256]{1,0:T(1,128)S(1)} %get-tuple-element.237) | copy-start | bytes 3076
  15.9 11.8 %copy-start.26 = (bf16[128,256]{1,0:T(8,128)(2,1)}, bf16[128,256]{1,0:T(8,128)(2,1)S(1)}, u32[]{:S(2)}) copy-start(bf16[128,256]{1,0:T(8,128)(2,1)S(1)} %get-tuple-element.245) | copy-start | bytes 196612
  17.9 9.9 copy-start.28
  20.0 7.8 copy-start.31
  22.1 5.7 copy-start.34
  25.3 17.0 %copy-start.2 = (bf16[1,1,8,256,256]{4,3,2,1,0:T(8,128)(2,1)S(1)}, bf16[1,1,8,256,256]{4,3,2,1,0:T(8,128)(2,1)}, u32[]{:S(2)}) copy-start(bf16[1,1,8,256,256]{4,3,2,1,0:T(8,128)(2,1)} %param.56) | copy-start | bytes 3145732
  28.6 15.8 %copy-start.1 = (bf16[1,1,8,256,256]{4,3,2,1,0:T(8,128)(2,1)S(1)}, bf16[1,1,8,256,256]{4,3,2,1,0:T(8,128)(2,1)}, u32[]{:S(2)}) copy-start(bf16[1,1,8,256,256]{4,3,2,1,0:T(8,128)(2,1)} %param.55) | copy-start | bytes 3145732
  31.2 101.4 %copy-start.9 = (bf16[1,1,256,256]{3,2,1,0:T(8,128)(2,1)S(1)}, bf16[1,1,256,256]{3,2,1,0:T(8,128)(2,1)}, u32[]{:S(2)}) copy-start(bf16[1,1,256,256]{3,2,1,0:T(8,128)(2,1)} %param.57) | copy-start | bytes 393220
  33.8 100.6 %copy-start.25 = (bf16[1,16,256]{2,1,0:T(8,128)(2,1)S(1)}, bf16[1,16,256]{2,1,0:T(8,128)(2,1)}, u32[]{:S(2)}) copy-start(bf16[1,16,256]{2,1,0:T(8,128)(2,1)} %param.58) | copy-start | bytes 24580
  33.8 209.2 %copy-start.8 = (bf16[1,256,256]{2,1,0:T(8,128)(2,1)S(1)}, bf16[1,256,256]{2,1,0:T(8,128)(2,1)}, u32[]{:S(2)}) copy-start(bf16[1,256,256]{2,1,0:T(8,128)(2,1)} %param.51) | copy-start | bytes 393220
  33.8 456.4 %copy-start.10 = (bf16[256,256]{1,0:T(8,128)(2,1)S(1)}, bf16[256,256]{1,0:T(8,128)(2,1)}, u32[]{:S(2)}) copy-start(bf16[256,256]{1,0:T(8,128)(2,1)} %param.52) | copy-start | bytes 393220
  36.0 207.0 %all-reduce.11.cloned.1.call-start = ((), (), s32[]{:S(2)}) async-start(), calls=%async_computation.1 | async-start | bytes 262144 | tf_op jit(solution)/shard_map/psum | solution.py:127
  134.4 355.9 %all-reduce.13.cloned.1.call-start = ((), (), s32[]{:S(2)}) async-start(), calls=%async_computation.2 | async-start | bytes 262144 | tf_op jit(solution)/shard_map/psum | solution.py:131
  246.6 337.7 %all-reduce.15.cloned.1.call-start = ((), (), s32[]{:S(2)}) async-start(), calls=%async_computation.3 | async-start | bytes 262144 | tf_op jit(solution)/shard_map/psum | solution.py:143
  495.7 214.0 %all-reduce.17.cloned.1.call-start = ((), (), s32[]{:S(2)}) async-start(), calls=%async_computation.4 | async-start | bytes 262144 | tf_op jit(solution)/shard_map/psum | solution.py:122
  584.2 3.6 copy-start.12
  586.4 1.8 copy-start.6
  586.4 1.8 copy-start.42
  586.5 1.8 copy-start.58
  586.5 2.4 copy-start.3
  586.5 2.4 copy-start.70
  588.2 1.9 copy-start.38
  588.2 1.9 copy-start.52
  588.2 2.0 copy-start.68
  588.9 1.7 copy-start.18
  588.9 1.7 copy-start.36
  588.9 1.7 copy-start.49
  588.9 1.8 copy-start.66
  589.2 1.8 copy-start.35
  589.2 1.8 copy-start.46
  589.4 1.8 copy-start.64
  589.4 2.4 copy-start.32
  590.0 1.9 copy-start.72
  590.0 2.2 copy-start.29
  590.2 2.2 copy-start.19
  590.2 2.8 copy-start.27
  590.2 2.8 copy-start.62
  590.7 1.7 copy-start.20
  617.8 204.2 %all-reduce.19.cloned.1.call-start = ((), (), s32[]{:S(2)}) async-start(), calls=%async_computation.5 | async-start | bytes 262144 | tf_op jit(solution)/shard_map/psum | solution.py:127
  713.4 356.8 %all-reduce.21.cloned.1.call-start = ((), (), s32[]{:S(2)}) async-start(), calls=%async_computation.6 | async-start | bytes 262144 | tf_op jit(solution)/shard_map/psum | solution.py:131
  825.5 337.2 %all-reduce.23.cloned.1.call-start = ((), (), s32[]{:S(2)}) async-start(), calls=%async_computation.7 | async-start | bytes 262144 | tf_op jit(solution)/shard_map/psum | solution.py:143
  1073.3 94.4 %copy-start.11 = (bf16[128,256]{1,0:T(8,128)(2,1)S(1)}, bf16[128,256]{1,0:T(8,128)(2,1)}, u32[]{:S(2)}) copy-start(bf16[128,256]{1,0:T(8,128)(2,1)} %convolution_convert_fusion.2) | copy-start | bytes 196612
  1165.3 2.8 copy-start.44
  1165.3 2.8 copy-start.59
  1165.3 3.0 copy-start.71
  1166.1 2.1 copy-start.7
  1166.1 2.7 copy-start.4
  1169.3 1.7 copy-start.33
  1169.6 1.7 copy-start.30
  1169.8 1.7 copy-start.63
  1169.8 1.7 copy-start.76
  (29 other events, 32.8 us)
Sparse Core Ops, SparseCore 0:
  36.1 94.5 all-reduce.8
  134.5 108.4 all-reduce.10
  249.1 241.1 all-reduce.12
  495.8 88.3 all-reduce.14
  617.9 91.7 all-reduce.16
  713.5 108.4 all-reduce.18
  829.0 241.1 all-reduce.20
  1074.3 88.4 all-reduce.22
where the time goes:
time: 1180 us
  waiting for transfers between devices  1010 us (86%)
  matrix products  92.7 us (8%)
  blocking collectives  38.1 us (3%)
  local copies, waits for them, and re-layouts  23.6 us (2%)
  between operations  16.2 us (1%)
    psum x2, waiting for transfers between devices, per_device(): lax.psum(summit_term + multiply(own_lift, own_strip, 'ki,kn->in'), ('prow...  487 us
    psum x2, waiting for transfers between devices, per_device(): strip_partial = lax.psum(strip_term, 'prow')  213 us
    psum x2, waiting for transfers between devices, per_device(): band_partial = lax.psum(band_term, 'pcol')  174 us
    psum x2, waiting for transfers between devices, per_device(): lax.psum(downward, 'pcol')  132 us
    dot_general x76, matrix products, multiply(): return jnp.einsum(form, left, right, preferred_element_type=jnp.float32)  92.7 us
    all_gather x2, blocking collectives, per_device(): lax.all_gather(band_piece, 'pcol', axis=0, tiled=True)  38.1 us
  transfers between devices with their start and end apart: 8, of which 8 were waited for; matrix products, arithmetic and copies ran while one was open for 2% of the time, Pallas kernels for 0%

commit v1 on v0

v1 whole, which is shorter than its diff:
```python
import functools

import jax
import jax.numpy as jnp
from jax import lax
from jax.experimental import pallas as pl
from jax.experimental.pallas import tpu as pltpu
from jax.sharding import PartitionSpec as P

PASSES = 2
MESH = pl.DeviceIdType.MESH
F32 = jnp.float32
BF16 = jnp.bfloat16


def nn(left, right):
    return jnp.dot(left, right, preferred_element_type=F32)


def nt(left, right):
    return lax.dot_general(left, right, (((1,), (1,)), ((), ())), preferred_element_type=F32)


def pair(a, b):
    return a * (a - 1) // 2 + b


def kernel(
    rows,
    cols,
    parents,
    widths,
    leaf_source,
    band_source,
    strip_source,
    summit_source,
    leaf_inverse,
    band_inverse,
    strip_inverse,
    summit_inverse,
    leaf_blocks,
    band_blocks,
    strip_blocks,
    summit_blocks,
    coupling,
    summit_band,
    summit_strip,
    leaf_out,
    band_out,
    strip_out,
    summit_out,
    source_in,
    border_in,
    linv,
    lblk,
    bblk,
    sblk,
    mblk,
    link,
    binv,
    sinv,
    uinv,
    lift_in,
    lift,
    slift,
    now,
    solved,
    pend,
    band_src,
    strip_src,
    summit_src,
    send1,
    send3,
    send6,
    land1,
    land2,
    land3,
    land4,
    land5,
    land6,
    land7,
    band_hold,
    load_sem,
    send_sem,
    recv_sem,
):
    leaves, size, count = leaf_source.shape
    r = lax.axis_index("prow")
    c = lax.axis_index("pcol")
    band_rhs = count // cols
    strip_rhs = count // rows

    loads = [
        (leaf_source, source_in),
        (leaf_inverse, linv),
        (leaf_blocks, lblk),
        (band_blocks, bblk),
        (strip_blocks, sblk),
        (summit_blocks, mblk),
        (band_source, border_in.at[0]),
        (strip_source, border_in.at[1]),
        (summit_source, border_in.at[2]),
        (coupling, link),
        (band_inverse, binv),
        (strip_inverse, sinv),
        (summit_inverse, uinv),
        (summit_band, lift_in),
        (summit_strip, slift),
    ]
    copies = [
        pltpu.make_async_copy(src, dst, load_sem.at[place])
        for place, (src, dst) in enumerate(loads)
    ]
    for copy in copies:
        copy.start()

    barrier = pltpu.get_barrier_semaphore()

    def greet_col(k, carry):
        pl.semaphore_signal(
            barrier, inc=1, device_id=(r, lax.rem(c + k, cols)), device_id_type=MESH
        )
        return carry

    def greet_row(k, carry):
        pl.semaphore_signal(
            barrier, inc=1, device_id=(lax.rem(r + k, rows), c), device_id_type=MESH
        )
        return carry

    lax.fori_loop(1, cols, greet_col, 0)
    lax.fori_loop(1, rows, greet_row, 0)

    def reach_of():
        parent = [parents[b] for b in range(leaves)]
        reach = {}
        for a in range(leaves):
            for b in reversed(range(a)):
                met = (parent[b] == a).astype(jnp.int32)
                for k in range(b + 1, a):
                    met = met + (parent[b] == k).astype(jnp.int32) * reach[a, k]
                reach[a, b] = met
        return reach

    reach = reach_of()

    copies[0].wait()
    for a in range(leaves):
        now[a] = source_in[a].astype(F32).T.astype(BF16)
    copies[1].wait()
    down = lax.broadcasted_iota(jnp.int32, (size, size), 0)
    across = lax.broadcasted_iota(jnp.int32, (size, size), 1)
    furthest = jnp.maximum(down, across)
    for a in range(leaves):
        linv[a] = jnp.where(furthest < widths[a], linv[a].astype(F32), 0.0).astype(BF16)
    copies[2].wait()
    for a in range(leaves):
        for b in range(a):
            weight = reach[a, b].astype(F32)
            lblk[pair(a, b)] = (lblk[pair(a, b)].astype(F32) * weight).astype(BF16)
    for copy in copies[3:]:
        copy.wait()
    send1[...] = border_in[0].astype(F32).T.reshape(send1.shape)
    band_src[...] = send1[c]
    send3[:, 0] = border_in[1].astype(F32).T.reshape(rows, strip_rhs, size)
    send3[:, 1] = border_in[2].astype(F32).T.reshape(rows, strip_rhs, size)
    strip_src[...] = send3[r, 0]
    summit_src[...] = send3[r, 1]
    lift[...] = jnp.zeros_like(lift)
    slab = lift_in.shape[0]
    lift[pl.ds(pl.multiple_of(c * slab, slab), slab), :] = lift_in[...]

    def col_copy(p, phase, src, dst, other):
        return pltpu.make_async_remote_copy(
            src_ref=src,
            dst_ref=dst,
            send_sem=send_sem.at[p, phase],
            recv_sem=recv_sem.at[p, phase],
            device_id=(r, other),
            device_id_type=MESH,
        )

    def row_copy(p, phase, src, dst, other):
        return pltpu.make_async_remote_copy(
            src_ref=src,
            dst_ref=dst,
            send_sem=send_sem.at[p, phase],
            recv_sem=recv_sem.at[p, phase],
            device_id=(other, c),
            device_id_type=MESH,
        )

    def scatter(make, p, phase, me, n, source, land):
        def step(k, carry):
            other = lax.rem(me + k, n)
            make(p, phase, source.at[other], land.at[p, me], other).start()
            return carry

        lax.fori_loop(1, n, step, 0)
        land[p, me] = source[me]

    def spread(make, p, phase, me, n, land):
        def step(k, carry):
            other = lax.rem(me + k, n)
            make(p, phase, land.at[p, me], land.at[p, me], other).start()
            return carry

        lax.fori_loop(1, n, step, 0)

    def finish(make, p, phase, n, land):
        part = land.at[p, pl.ds(0, n - 1)]
        copy = make(p, phase, part, part, 0)
        copy.wait_recv()
        copy.wait_send()

    def total(values):
        values = [values[k] for k in range(values.shape[0])]
        while len(values) > 1:
            values = [
                values[k] + values[k + 1] if k + 1 < len(values) else values[k]
                for k in range(0, len(values), 2)
            ]
        return values[0]

    def full(value):
        return value.reshape(count, size).astype(BF16)

    def one_pass(p, carry):
        for a in range(leaves):
            pend[a] = now[a].astype(F32)
        for b in range(leaves):
            answer = nt(pend[b].astype(BF16), linv[b]).astype(BF16)
            solved[b] = answer
            for a in range(b + 1, leaves):
                pend[a] -= nt(answer, lblk[pair(a, b)])

        def term(blocks):
            result = nt(solved[0], blocks[0])
            for a in range(1, leaves):
                result = result + nt(solved[a], blocks[a])
            return result

        send1[...] = term(bblk).reshape(send1.shape)

        @pl.when(p == 0)
        def _():
            pl.semaphore_wait(barrier, rows + cols - 2)

        scatter(col_copy, p, 0, c, cols, send1, land1)
        strip_term = term(sblk)
        finish(col_copy, p, 0, cols, land1)
        rest = (band_src[...] - total(land1[p])).astype(BF16)
        band_slab = nt(rest, binv[...]).astype(BF16).astype(F32)
        band_hold[...] = band_slab
        land2[p, c] = band_slab
        spread(col_copy, p, 1, c, cols, land2)
        summit_term = term(mblk)
        finish(col_copy, p, 1, cols, land2)
        band_solved = full(land2[p])
        send3[:, 0] = (strip_term + nt(band_solved, link[...])).reshape(rows, strip_rhs, size)
        send3[:, 1] = (summit_term + nn(band_solved, lift[...])).reshape(rows, strip_rhs, size)
        scatter(row_copy, p, 2, r, rows, send3, land3)
        finish(row_copy, p, 2, rows, land3)
        sums = total(land3[p])
        strip_slab = nt((strip_src[...] - sums[0]).astype(BF16), sinv[...]).astype(BF16)
        land4[p, c] = sums[1] + nn(strip_slab, slift[...])
        spread(col_copy, p, 3, c, cols, land4)
        finish(col_copy, p, 3, cols, land4)
        top = nt((summit_src[...] - total(land4[p])).astype(BF16), uinv[...]).astype(BF16)
        top_answer = nn(top, uinv[...]).astype(BF16)
        rest = (strip_slab.astype(F32) - nt(top_answer, slift[...])).astype(BF16)
        strip_answer = nn(rest, sinv[...]).astype(BF16).astype(F32)
        top_answer = top_answer.astype(F32)
        strip_src[...] = strip_answer
        summit_src[...] = top_answer
        land5[p, r, 0] = strip_answer
        land5[p, r, 1] = top_answer
        spread(row_copy, p, 4, r, rows, land5)
        finish(row_copy, p, 4, rows, land5)
        strip_all = full(land5[p, :, 0])
        top_all = full(land5[p, :, 1])
        send6[...] = (nn(strip_all, link[...]) + nt(top_all, lift[...])).reshape(send6.shape)
        scatter(col_copy, p, 5, c, cols, send6, land6)
        for a in range(leaves):
            pend[a] = solved[a].astype(F32) - (nn(strip_all, sblk[a]) + nn(top_all, mblk[a]))
        finish(col_copy, p, 5, cols, land6)
        rest = (band_hold[...] - total(land6[p])).astype(BF16)
        band_answer = nn(rest, binv[...]).astype(BF16).astype(F32)
        band_src[...] = band_answer
        land7[p, c] = band_answer
        spread(col_copy, p, 6, c, cols, land7)
        finish(col_copy, p, 6, cols, land7)
        band_all = full(land7[p])
        for a in reversed(range(leaves)):
            pend[a] -= nn(band_all, bblk[a])
        for a in reversed(range(leaves)):
            answer = nn(pend[a].astype(BF16), linv[a]).astype(BF16)
            now[a] = answer
            for b in reversed(range(a)):
                pend[b] -= nn(answer, lblk[pair(a, b)])
        return carry

    lax.fori_loop(0, PASSES, one_pass, 0)
    last = PASSES - 1
    for a in range(leaves):
        leaf_out[a] = now[a].astype(F32).T.astype(BF16)
    band_out[...] = land7[last].reshape(count, size).T.astype(BF16)
    strip_out[...] = land5[last, :, 0].reshape(count, size).T.astype(BF16)
    summit_out[...] = land5[last, :, 1].reshape(count, size).T.astype(BF16)


def per_device(
    rows,
    cols,
    leaf_source,
    band_source,
    strip_source,
    summit_source,
    leaf_inverse,
    band_inverse,
    strip_inverse,
    summit_inverse,
    leaf_blocks,
    band_blocks,
    strip_blocks,
    summit_blocks,
    coupling,
    summit_band,
    summit_strip,
    parents,
    widths,
):
    leaves, size, count = leaf_source.shape[2:]
    pairs = leaf_blocks.shape[2]
    slab = summit_band.shape[1]
    band_rhs = count // cols
    strip_rhs = count // rows
    square = (size, size)
    anywhere = pl.BlockSpec(memory_space=pl.ANY)
    scalars = pl.BlockSpec(memory_space=pltpu.SMEM)
    vmem = pl.BlockSpec(memory_space=pltpu.VMEM)
    results = pl.pallas_call(
        functools.partial(kernel, rows, cols),
        out_shape=(
            jax.ShapeDtypeStruct((leaves, size, count), BF16),
            jax.ShapeDtypeStruct((size, count), BF16),
            jax.ShapeDtypeStruct((size, count), BF16),
            jax.ShapeDtypeStruct((size, count), BF16),
        ),
        in_specs=[scalars] * 2 + [anywhere] * 15,
        out_specs=(vmem,) * 4,
        scratch_shapes=[
            pltpu.VMEM((leaves, size, count), BF16),
            pltpu.VMEM((3, size, count), BF16),
            pltpu.VMEM((leaves,) + square, BF16),
            pltpu.VMEM((pairs,) + square, BF16),
            pltpu.VMEM((leaves,) + square, BF16),
            pltpu.VMEM((leaves,) + square, BF16),
            pltpu.VMEM((leaves,) + square, BF16),
            pltpu.VMEM(square, BF16),
            pltpu.VMEM(square, BF16),
            pltpu.VMEM(square, BF16),
            pltpu.VMEM(square, BF16),
            pltpu.VMEM((slab, size), BF16),
            pltpu.VMEM(square, BF16),
            pltpu.VMEM(square, BF16),
            pltpu.VMEM((leaves, count, size), BF16),
            pltpu.VMEM((leaves, count, size), BF16),
            pltpu.VMEM((leaves, count, size), F32),
            pltpu.VMEM((band_rhs, size), F32),
            pltpu.VMEM((strip_rhs, size), F32),
            pltpu.VMEM((strip_rhs, size), F32),
            pltpu.VMEM((cols, band_rhs, size), F32),
            pltpu.VMEM((rows, 2, strip_rhs, size), F32),
            pltpu.VMEM((cols, band_rhs, size), F32),
            pltpu.VMEM((PASSES, cols, band_rhs, size), F32),
            pltpu.VMEM((PASSES, cols, band_rhs, size), F32),
            pltpu.VMEM((PASSES, rows, 2, strip_rhs, size), F32),
            pltpu.VMEM((PASSES, cols, strip_rhs, size), F32),
            pltpu.VMEM((PASSES, rows, 2, strip_rhs, size), F32),
            pltpu.VMEM((PASSES, cols, band_rhs, size), F32),
            pltpu.VMEM((PASSES, cols, band_rhs, size), F32),
            pltpu.VMEM((band_rhs, size), F32),
            pltpu.SemaphoreType.DMA((15,)),
            pltpu.SemaphoreType.DMA((PASSES, 7)),
            pltpu.SemaphoreType.DMA((PASSES, 7)),
        ],
        compiler_params=pltpu.CompilerParams(
            collective_id=0, has_side_effects=True, vmem_limit_bytes=56 * 1024 * 1024
        ),
        cost_estimate=pl.CostEstimate(
            flops=4_400_000_000, bytes_accessed=10_000_000, transcendentals=0
        ),
    )(
        parents[0, 0],
        widths[0, 0],
        leaf_source[0, 0],
        band_source[0],
        strip_source[0],
        summit_source,
        leaf_inverse[0, 0],
        band_inverse[0],
        strip_inverse[0],
        summit_inverse,
        leaf_blocks[0, 0],
        band_blocks[0, 0],
        strip_blocks[0, 0],
        summit_blocks[0, 0],
        coupling[0, 0],
        summit_band[0],
        summit_strip[0],
    )
    return results[0][None, None], results[1][None], results[2][None], results[3]


def solution(mesh):
    placed = (
        P("prow", "pcol", None, None, None),
        P("prow", None, None),
        P("pcol", None, None),
        P(),
        P("prow", "pcol", None, None, None),
        P("prow", None, None),
        P("pcol", None, None),
        P(),
        P("prow", "pcol", None, None, None),
        P("prow", "pcol", None, None, None),
        P("prow", "pcol", None, None, None),
        P("prow", "pcol", None, None, None),
        P("prow", "pcol", None, None),
        P("prow", "pcol", None),
        P("pcol", None, None),
        P("prow", "pcol", None),
        P("prow", "pcol", None),
    )
    return jax.shard_map(
        functools.partial(per_device, mesh.shape["prow"], mesh.shape["pcol"]),
        mesh=mesh,
        in_specs=placed,
        out_specs=(
            P("prow", "pcol", None, None, None),
            P("prow", None, None),
            P("pcol", None, None),
            P(),
        ),
        check_vma=False,
    )
```

time: 1180 us -> 112 us (0.09)
  waiting for transfers between devices: 1010 us -> 0 us
  Pallas kernels: 0 us -> 105 us
  matrix products: 92.7 us -> 0 us
  blocking collectives: 38.1 us -> 0 us
  local copies, waits for them, and re-layouts: 23.6 us -> 6.29 us
  between operations: 16.2 us -> 0.65 us
    psum x8 -> x0, waiting for transfers between devices: 1010 us -> none  [the longest x2 487 us: per_device(): lax.psum(summit_term + multiply(own_lift, own_strip, 'ki,kn->in'), ('prow...]
    pallas_call x0 -> x1, Pallas kernels: none -> 105 us  [per_device(): pl.pallas_call(functools.partial(kernel, rows, cols), out_shape=(jax.Shap...]
    dot_general x76 -> x0, matrix products: 92.7 us -> none  [multiply(): return jnp.einsum(form, left, right, preferred_element_type=jnp.float32)]
    all_gather x2 -> x0, blocking collectives: 38.1 us -> none  [per_device(): lax.all_gather(band_piece, 'pcol', axis=0, tiled=True)]
  transfers between devices with their start and end apart: 8 -> 0, of which waited for: 8 -> 0; matrix products, arithmetic and copies ran while one was open for 2% -> 0% of each run, Pallas kernels for 0% -> 0%
where the time goes in v1:
time: 112 us
  Pallas kernels  105 us (94%)
  local copies, waits for them, and re-layouts  6.29 us (6%)
    pallas_call x1, Pallas kernels, per_device(): pl.pallas_call(functools.partial(kernel, rows, cols), out_shape=(jax.Shap...  105 us
    unnamed x4, local copies, waits for them, and re-layouts  6.29 us

profile of v1, /device:TPU:1, one launch (start us, length us, event | category | flops | bytes accessed | tf_op | source)
XLA Modules:
  0.0 111.8 jit_solution(16857049090314831793)
XLA Ops:
  0.6 104.8 %shard_map.192 = (bf16[8,256,128]{2,1,0:T(8,128)(2,1)}, bf16[256,128]{1,0:T(8,128)(2,1)}, bf16[256,128]{1,0:T(8,128)(2,1)}, bf16[256,128]{1,0:T(8,128)(2,1)}) custom-call(s32[8]{0:T(128)} %bitcast.34, s32[8]{0:T(128)} %bitcast.35, bf16[8,256,128]{2,1,0:T(8,128)(2,1)} %bitcast.26, bf16[256,128]{1,0:T(8,128)(2,1)} %bitcast.31, bf16[256,128]{1,0:T(8,128)(2,1)} %bitcast.32, ...), custom_call_target="tpu_custom_call" | custom-call | flops 4400000000 | bytes 10000000 | tf_op jit(solution)/shard_map/pallas_call | solution.py:342
  105.5 1.9 %copy.25 = bf16[1,1,8,256,128]{4,3,2,1,0:T(8,128)(2,1)} copy(bf16[1,1,8,256,128]{4,3,2,1,0:T(8,128)(2,1)} %bitcast.18) | data formatting | bytes 1048576
  107.3 1.5 %copy.26 = bf16[1,256,128]{2,1,0:T(8,128)(2,1)} copy(bf16[1,256,128]{2,1,0:T(8,128)(2,1)} %bitcast.20) | data formatting | bytes 131072
  108.8 1.5 %copy.27 = bf16[1,256,128]{2,1,0:T(8,128)(2,1)} copy(bf16[1,256,128]{2,1,0:T(8,128)(2,1)} %bitcast.19) | data formatting | bytes 131072
  110.3 1.5 %copy.28 = bf16[256,128]{1,0:T(8,128)(2,1)} copy(bf16[256,128]{1,0:T(8,128)(2,1)} %get-tuple-element.19) | data formatting | bytes 131072

commit v2 on v1

v2 whole, which is shorter than its diff:
```python
import functools

import jax
import jax.numpy as jnp
from jax import lax
from jax.experimental import pallas as pl
from jax.experimental.pallas import tpu as pltpu
from jax.sharding import PartitionSpec as P

PASSES = 2
MESH = pl.DeviceIdType.MESH
F32 = jnp.float32
BF16 = jnp.bfloat16


def nn(left, right):
    return jnp.dot(left, right, preferred_element_type=F32)


def nt(left, right):
    return lax.dot_general(left, right, (((1,), (1,)), ((), ())), preferred_element_type=F32)


def pair(a, b):
    return a * (a - 1) // 2 + b


def kernel(
    rows,
    cols,
    parents,
    widths,
    leaf_source,
    band_source,
    strip_source,
    summit_source,
    leaf_inverse,
    band_inverse,
    strip_inverse,
    summit_inverse,
    leaf_blocks,
    band_blocks,
    strip_blocks,
    summit_blocks,
    coupling,
    summit_band,
    summit_strip,
    leaf_out,
    border_out,
    source_in,
    border_in,
    linv,
    lblk,
    stack,
    keys,
    link,
    binv,
    sinv,
    uinv,
    lift_in,
    lift,
    slift,
    lowered,
    joined,
    now,
    solved,
    pend,
    slabs,
    sends,
    send_mats,
    send_pair,
    lands,
    land_mats,
    land_pair,
    load_sem,
    send_sem,
    recv_sem,
):
    leaves, size, count = leaf_source.shape
    r = lax.axis_index("prow")
    c = lax.axis_index("pcol")

    side = int(round(cols**0.5))
    chips = rows // 2

    def away(step, n):
        return min(step, n - step)

    col_steps = sorted(
        range(1, cols), key=lambda k: -away(k // side, side) - away(k % side, side)
    )
    row_steps = sorted(range(1, rows), key=lambda k: -away(k // 2, chips))
    col_peers = [
        (r, lax.rem(c // side + k // side, side) * side + lax.rem(c % side + k % side, side))
        for k in col_steps
    ]
    row_peers = [
        (lax.rem(r // 2 + k // 2, chips) * 2 + lax.rem(r % 2 + k % 2, 2), c) for k in row_steps
    ]
    along_cols = (1, c, col_peers)
    along_rows = (0, r, row_peers)

    def whole(place):
        return stack.at[:, pl.ds(place * size, size), :]

    loads = [(leaf_source, source_in), (leaf_inverse, linv)]
    for a in range(1, leaves):
        part = pl.ds(pair(a, 0), a)
        loads.append((leaf_blocks.at[part], lblk.at[part]))
    loads += [
        (band_blocks, whole(0)),
        (strip_blocks, whole(1)),
        (summit_blocks, whole(2)),
        (band_source, border_in.at[0]),
        (strip_source, border_in.at[1]),
        (summit_source, border_in.at[2]),
        (coupling, link),
        (band_inverse, binv),
        (strip_inverse, sinv),
        (summit_inverse, uinv),
        (summit_band, lift_in),
        (summit_strip, slift),
    ]
    copies = [
        pltpu.make_async_copy(src, dst, load_sem.at[place])
        for place, (src, dst) in enumerate(loads)
    ]
    for copy in copies:
        copy.start()

    barrier = pltpu.get_barrier_semaphore()
    for peer in col_peers + row_peers:
        pl.semaphore_signal(barrier, inc=1, device_id=peer, device_id_type=MESH)

    parent = [parents[b] for b in range(leaves)]
    reach = {}
    for a in range(leaves):
        for b in reversed(range(a)):
            met = (parent[b] == a).astype(jnp.int32)
            for k in range(b + 1, a):
                met = met + (parent[b] == k).astype(jnp.int32) * reach[a, k]
            reach[a, b] = met
    down = lax.broadcasted_iota(jnp.int32, (size, size), 0)
    across = lax.broadcasted_iota(jnp.int32, (size, size), 1)
    furthest = jnp.maximum(down, across)

    def prepare(a):
        linv[a] = jnp.where(furthest < widths[a], linv[a].astype(F32), 0.0).astype(BF16)
        now[a] = source_in[a].astype(F32).T.astype(BF16)
        for b in range(a):
            weight = reach[a, b].astype(F32)
            lblk[pair(a, b)] = (lblk[pair(a, b)].astype(F32) * weight).astype(BF16)

    used = []

    def ship(make_src, make_dst, peers, phase):
        for peer in peers:
            pltpu.make_async_remote_copy(
                src_ref=make_src(peer),
                dst_ref=make_dst(peer),
                send_sem=send_sem.at[phase],
                recv_sem=recv_sem.at[phase],
                device_id=peer,
                device_id_type=MESH,
            ).start()

    def scatter(axis, phase, source, land):
        dim, me, peers = axis
        ship(lambda peer: source.at[peer[dim]], lambda peer: land.at[me], peers, phase)
        land[me] = source[me]
        used.append((peers, land, phase))

    def spread(axis, phase, value, land):
        dim, me, peers = axis
        land[me] = value
        ship(lambda peer: land.at[me], lambda peer: land.at[me], peers, phase)
        used.append((peers, land, phase))

    def bytes_of(peers, land, phase):
        part = land.at[pl.ds(0, len(peers))]
        return pltpu.make_async_remote_copy(
            src_ref=part,
            dst_ref=part,
            send_sem=send_sem.at[phase],
            recv_sem=recv_sem.at[phase],
            device_id=peers[0],
            device_id_type=MESH,
        )

    def finish(axis, phase, land):
        bytes_of(axis[2], land, phase).wait_recv()

    def total(values):
        values = [values[k] for k in range(values.shape[0])]
        while len(values) > 1:
            values = [
                values[k] + values[k + 1] if k + 1 < len(values) else values[k]
                for k in range(0, len(values), 2)
            ]
        return values[0]

    def full(value):
        return value.reshape(count, size).astype(BF16)

    def parts(value, n):
        return value.reshape(n, count // n, size)

    def rounded(value):
        return value.astype(BF16).astype(F32)

    def forward_step(a):
        rest = now[a].astype(F32)
        for b in range(a):
            rest = rest - nt(solved[b], lblk[pair(a, b)])
        solved[a] = nt(rest.astype(BF16), linv[a]).astype(BF16)

    def backward_chain():
        for a in reversed(range(leaves)):
            rest = solved[a].astype(F32)
            for b in range(a + 1, leaves):
                rest = rest - nn(solved[b], lblk[pair(b, a)])
            answer = nn(rest.astype(BF16), linv[a])
            pend[a] = answer
            solved[a] = answer.astype(BF16)

    def term(values, blocks, place):
        part = pl.ds(place * size, size)
        result = nt(values[0], blocks[0, part, :])
        for a in range(1, leaves):
            result = result + nt(values[a], blocks[a, part, :])
        return result

    copies[0].wait()
    copies[1].wait()
    prepare(0)
    for a in range(leaves):
        if a + 1 < leaves:
            copies[2 + a].wait()
            prepare(a + 1)
        forward_step(a)
    for copy in copies[leaves + 1 :]:
        copy.wait()
    sends[0] = parts(term(solved, stack, 0), cols)
    pl.semaphore_wait(barrier, rows + cols - 2)
    scatter(along_cols, 0, sends.at[0], lands.at[0])

    strip_term = term(solved, stack, 1)
    summit_term = term(solved, stack, 2)
    slabs[0] = parts(border_in[0].astype(F32).T, cols)
    slabs[1] = parts(border_in[1].astype(F32).T, rows)
    slabs[2] = parts(border_in[2].astype(F32).T, cols)
    band_src = slabs[0, c]
    strip_src = slabs[1, r]
    summit_src = slabs[2, c]
    strip_now = slabs[1].reshape(count, size)
    lift[...] = jnp.zeros_like(lift)
    slab = lift_in.shape[0]
    lift[pl.ds(pl.multiple_of(c * slab, slab), slab), :] = lift_in[...]
    turned = sinv[...].astype(F32).T.astype(BF16)
    lowered[...] = nn(turned, slift[...]).astype(BF16)
    joined[...] = nn(sinv[...], link[...]).astype(BF16)
    turned = link[...].astype(F32).T.astype(BF16)
    send_mats[:, 0] = (nn(turned, lowered[...]) - lift[...].astype(F32)).reshape(cols, slab, size)

    def key_step(a):
        rest = stack[a].astype(F32)
        for b in range(a + 1, leaves):
            rest = rest - nn(keys[b], lblk[pair(b, a)])
        keys[a] = nn(rest.astype(BF16), linv[a]).astype(BF16)

    half = leaves // 2
    for a in reversed(range(half, leaves)):
        key_step(a)
    finish(along_cols, 0, lands.at[0])
    rest = band_src - total(lands[0])
    band_slab = rounded(nt(rest.astype(BF16), binv[...]))
    spread(along_cols, 1, band_slab, lands.at[1])
    for a in reversed(range(half)):
        key_step(a)
    cross = nt(keys[0, pl.ds(0, size), :], keys[0])
    for a in range(1, leaves):
        cross = cross + nt(keys[a, pl.ds(0, size), :], keys[a])
    band_strip = cross[:, size : 2 * size].astype(BF16)
    send_mats[:, 1] = cross[:, :size].reshape(cols, slab, size)
    send_mats[:, 2] = (nn(band_strip, lowered[...]) - cross[:, 2 * size :]).reshape(
        cols, slab, size
    )
    finish(along_cols, 1, lands.at[1])
    band_all = full(lands[1])

    mats = None
    for p in range(PASSES):
        first = p == 0
        base = 2 + 7 * p
        pushed = strip_term + nt(band_all, link[...])
        sends[base] = parts(pushed, rows)
        scatter(along_rows, base, sends.at[base], lands.at[base])
        spare = (strip_now * (1.0 / rows) - pushed).astype(BF16)
        if not first:
            summit_term = term(now, keys, 2)
        raised = summit_term + nn(band_all, lift[...]) + nn(spare, lowered[...])
        sends[base + 1] = parts(raised, cols)
        scatter(along_cols, base + 1, sends.at[base + 1], lands.at[base + 1])
        if first:
            mat_phase = 2 + 7 * PASSES
            scatter(along_cols, mat_phase, send_mats, land_mats.at[0])
        else:
            for a in range(leaves):
                forward_step(a)
        backward_chain()
        finish(along_rows, base, lands.at[base])
        rest = strip_src - total(lands[base])
        strip_slab = rounded(nt(rest.astype(BF16), sinv[...]))
        spread(along_rows, base + 2, strip_slab, lands.at[base + 2])
        finish(along_cols, base + 1, lands.at[base + 1])
        spread(along_rows, base + 3, total(lands[base + 1]), lands.at[base + 3])
        if first:
            finish(along_cols, mat_phase, land_mats.at[0])
            spread(along_cols, mat_phase + 1, total(land_mats[0]), land_mats.at[1])
            next_term = term(solved, keys, 0)
        finish(along_rows, base + 2, lands.at[base + 2])
        strip_all = full(lands[base + 2])
        dropped = nn(strip_all, joined[...])
        strip_own = nn(strip_all, sinv[...])
        if first:
            send_pair[:, 0] = parts(dropped, cols)
            send_pair[:, 1] = parts(next_term - nt(strip_own.astype(BF16), band_strip), cols)
            scatter(along_cols, base + 4, send_pair, land_pair.at[0])
        else:
            sends[base + 4] = parts(dropped, cols)
            scatter(along_cols, base + 4, sends.at[base + 4], lands.at[base + 4])
        finish(along_rows, base + 3, lands.at[base + 3])
        rest = summit_src - total(lands[base + 3])
        top = nt(rest.astype(BF16), uinv[...]).astype(BF16)
        top = nn(top, uinv[...]).astype(BF16)
        summit_src = top.astype(F32)
        spread(along_cols, base + 5, summit_src, lands.at[base + 5])
        if first:
            finish(along_cols, mat_phase + 1, land_mats.at[1])
            mats = [land_mats[1, :, k].reshape(size, size).astype(BF16) for k in range(3)]
            lblk_back = nt(top, mats[2])
        back = nt(top, mats[0])
        if first:
            finish(along_cols, base + 4, land_pair.at[0])
            sums = total(land_pair[0])
            rest = band_slab - sums[0] + back
            band_answer = nn(rest.astype(BF16), binv[...]).astype(BF16)
            rest = band_answer.astype(F32) - sums[1] + nt(band_answer, mats[1]) - lblk_back
            band_slab = rounded(nt(rest.astype(BF16), binv[...]))
            both = jnp.stack([band_answer.astype(F32), band_slab])
            spread(along_cols, base + 6, both, land_pair.at[1])
        else:
            finish(along_cols, base + 4, lands.at[base + 4])
            rest = band_slab - total(lands[base + 4]) + back
            band_answer = rounded(nn(rest.astype(BF16), binv[...]))
            spread(along_cols, base + 6, band_answer, lands.at[base + 6])
        finish(along_cols, base + 5, lands.at[base + 5])
        top_all = full(lands[base + 5])
        strip_answer = (strip_own - nt(top_all, lowered[...])).astype(BF16)
        strip_now = strip_answer.astype(F32)
        if first:
            slabs[1] = parts(strip_now, rows)
            strip_src = slabs[1, r]
        upper = jnp.concatenate([strip_answer, top_all], axis=1)
        lower_rows = pl.ds(size, 2 * size)
        for a in range(leaves):
            pend[a] -= nn(upper, keys[a, lower_rows, :])
        if first:
            finish(along_cols, base + 6, land_pair.at[1])
            band_full = full(land_pair[1, :, 0])
            band_all = full(land_pair[1, :, 1])
        else:
            finish(along_cols, base + 6, lands.at[base + 6])
            band_full = full(lands[base + 6])
        place = pl.ds(0, size)
        for a in range(leaves):
            value = (pend[a] - nn(band_full, keys[a, place, :])).astype(BF16)
            if first:
                now[a] = value
            else:
                leaf_out[a] = value
        if first:
            strip_term = term(now, keys, 1)
    border_out[0] = band_full
    border_out[1] = strip_answer
    border_out[2] = top_all
    for peers, land, phase in used:
        bytes_of(peers, land, phase).wait_send()


def turn(leaf_in, border_in, leaf_out, band_out, strip_out, summit_out):
    for a in range(leaf_in.shape[0]):
        leaf_out[a] = leaf_in[a].astype(F32).T.astype(BF16)
    for place, out in enumerate((band_out, strip_out, summit_out)):
        out[...] = border_in[place].astype(F32).T.astype(BF16)


def per_device(
    rows,
    cols,
    leaf_source,
    band_source,
    strip_source,
    summit_source,
    leaf_inverse,
    band_inverse,
    strip_inverse,
    summit_inverse,
    leaf_blocks,
    band_blocks,
    strip_blocks,
    summit_blocks,
    coupling,
    summit_band,
    summit_strip,
    parents,
    widths,
):
    leaves, size, count = leaf_source.shape[2:]
    pairs = leaf_blocks.shape[2]
    slab = summit_band.shape[1]
    band_rhs = count // cols
    square = (size, size)
    anywhere = pl.BlockSpec(memory_space=pl.ANY)
    scalars = pl.BlockSpec(memory_space=pltpu.SMEM)
    vmem = pl.BlockSpec(memory_space=pltpu.VMEM)
    plain = pltpu.VMEM(square, BF16)
    phases = 4 + 7 * PASSES
    solved = pl.pallas_call(
        functools.partial(kernel, rows, cols),
        out_shape=(
            jax.ShapeDtypeStruct((leaves, count, size), BF16),
            jax.ShapeDtypeStruct((3, count, size), BF16),
        ),
        in_specs=[scalars] * 2 + [anywhere] * 15,
        out_specs=(vmem,) * 2,
        scratch_shapes=[
            pltpu.VMEM((leaves, size, count), BF16),
            pltpu.VMEM((3, size, count), BF16),
            pltpu.VMEM((leaves,) + square, BF16),
            pltpu.VMEM((pairs,) + square, BF16),
            pltpu.VMEM((leaves, 3 * size, size), BF16),
            pltpu.VMEM((leaves, 3 * size, size), BF16),
            plain,
            plain,
            plain,
            plain,
            pltpu.VMEM((slab, size), BF16),
            plain,
            plain,
            plain,
            plain,
            pltpu.VMEM((leaves, count, size), BF16),
            pltpu.VMEM((leaves, count, size), BF16),
            pltpu.VMEM((leaves, count, size), F32),
            pltpu.VMEM((3, cols, band_rhs, size), F32),
            pltpu.VMEM((phases, cols, band_rhs, size), F32),
            pltpu.VMEM((cols, 3, slab, size), F32),
            pltpu.VMEM((cols, 2, band_rhs, size), F32),
            pltpu.VMEM((phases, cols, band_rhs, size), F32),
            pltpu.VMEM((2, cols, 3, slab, size), F32),
            pltpu.VMEM((2, cols, 2, band_rhs, size), F32),
            pltpu.SemaphoreType.DMA((32,)),
            pltpu.SemaphoreType.DMA((phases,)),
            pltpu.SemaphoreType.DMA((phases,)),
        ],
        compiler_params=pltpu.CompilerParams(
            collective_id=0, has_side_effects=True, vmem_limit_bytes=56 * 1024 * 1024
        ),
        cost_estimate=pl.CostEstimate(
            flops=4_400_000_000, bytes_accessed=10_000_000, transcendentals=0
        ),
    )(
        parents[0, 0],
        widths[0, 0],
        leaf_source[0, 0],
        band_source[0],
        strip_source[0],
        summit_source,
        leaf_inverse[0, 0],
        band_inverse[0],
        strip_inverse[0],
        summit_inverse,
        leaf_blocks[0, 0],
        band_blocks[0, 0],
        strip_blocks[0, 0],
        summit_blocks[0, 0],
        coupling[0, 0],
        summit_band[0],
        summit_strip[0],
    )
    results = pl.pallas_call(
        turn,
        out_shape=(
            jax.ShapeDtypeStruct((leaves, size, count), BF16),
            jax.ShapeDtypeStruct((size, count), BF16),
            jax.ShapeDtypeStruct((size, count), BF16),
            jax.ShapeDtypeStruct((size, count), BF16),
        ),
        in_specs=[vmem] * 2,
        out_specs=(vmem,) * 4,
    )(*solved)
    return results[0][None, None], results[1][None], results[2][None], results[3]


def solution(mesh):
    placed = (
        P("prow", "pcol", None, None, None),
        P("prow", None, None),
        P("pcol", None, None),
        P(),
        P("prow", "pcol", None, None, None),
        P("prow", None, None),
        P("pcol", None, None),
        P(),
        P("prow", "pcol", None, None, None),
        P("prow", "pcol", None, None, None),
        P("prow", "pcol", None, None, None),
        P("prow", "pcol", None, None, None),
        P("prow", "pcol", None, None),
        P("prow", "pcol", None),
        P("pcol", None, None),
        P("prow", "pcol", None),
        P("prow", "pcol", None),
    )
    return jax.shard_map(
        functools.partial(per_device, mesh.shape["prow"], mesh.shape["pcol"]),
        mesh=mesh,
        in_specs=placed,
        out_specs=(
            P("prow", "pcol", None, None, None),
            P("prow", None, None),
            P("pcol", None, None),
            P(),
        ),
        check_vma=False,
    )
```

time: 112 us -> 82 us (0.73)
  Pallas kernels: 105 us -> 81.3 us
  local copies, waits for them, and re-layouts: 6.29 us -> 0 us
    pallas_call x1, Pallas kernels: 105 us -> 79.1 us  [per_device(): pl.pallas_call(functools.partial(kernel, rows, cols), out_shape=(jax.Shap...]
    unnamed x4 -> x0, local copies, waits for them, and re-layouts: 6.29 us -> none
    pallas_call x0 -> x1, Pallas kernels: none -> 2.14 us  [per_device(): pl.pallas_call(turn, out_shape=(jax.ShapeDtypeStruct((leaves, size, count...]
where the time goes in v2:
time: 82 us; the launch traced here: 81.9 us
  Pallas kernels  81.3 us (99%)
    pallas_call x1, Pallas kernels, per_device(): pl.pallas_call(functools.partial(kernel, rows, cols), out_shape=(jax.Shap...  79.1 us
    pallas_call x1, Pallas kernels, per_device(): pl.pallas_call(turn, out_shape=(jax.ShapeDtypeStruct((leaves, size, count...  2.14 us

profile of v2, /device:TPU:1, one launch (start us, length us, event | category | flops | bytes accessed | tf_op | source)
XLA Modules:
  0.0 81.9 jit_solution(7019755497112239615)
XLA Ops:
  0.6 79.1 %shard_map.192 = (bf16[8,128,256]{2,1,0:T(8,128)(2,1)}, bf16[3,128,256]{2,1,0:T(8,128)(2,1)}) custom-call(s32[8]{0:T(128)} %bitcast.34, s32[8]{0:T(128)} %bitcast.35, bf16[8,256,128]{2,1,0:T(8,128)(2,1)} %bitcast.23, bf16[256,128]{1,0:T(8,128)(2,1)} %bitcast.29, bf16[256,128]{1,0:T(8,128)(2,1)} %bitcast.30, bf16[256,128]{1,0:T(8,128)(2,1)} %summit_source.1, ...), custom_call_target="tpu_custom_call" | custom-call | flops 4400000000 | bytes 10000000 | tf_op jit(solution)/shard_map/pallas_call | solution.py:429
  79.8 2.1 %shard_map.193 = (bf16[8,256,128]{2,1,0:T(8,128)(2,1)}, bf16[256,128]{1,0:T(8,128)(2,1)}, bf16[256,128]{1,0:T(8,128)(2,1)}, bf16[256,128]{1,0:T(8,128)(2,1)}) custom-call(bf16[8,128,256]{2,1,0:T(8,128)(2,1)} %get-tuple-element.10.leaf_in, bf16[3,128,256]{2,1,0:T(8,128)(2,1)} %get-tuple-element.11.border_in), custom_call_target="tpu_custom_call" | custom-call | tf_op jit(solution)/shard_map/pallas_call | solution.py:492

commit v3 on v2

--- a/solution.py
+++ b/solution.py
@@ -51,6 +51,7 @@
     border_in,
     linv,
     lblk,
+    bridge,
     stack,
     keys,
     link,
@@ -67,11 +68,16 @@
     pend,
     slabs,
     sends,
+    send_mat,
     send_mats,
     send_pair,
     lands,
+    land_mat,
     land_mats,
     land_pair,
+    land_twin,
+    ahead_all,
+    band_strip,
     load_sem,
     send_sem,
     recv_sem,
@@ -99,11 +105,20 @@
     ]
     along_cols = (1, c, col_peers)
     along_rows = (0, r, row_peers)
+    twin = (r + 1 - 2 * (r % 2), c)
+    along_chips = (0, r // 2, [peer for k, peer in zip(row_steps, row_peers) if k % 2 == 0])
 
     def whole(place):
         return stack.at[:, pl.ds(place * size, size), :]
 
-    loads = [(leaf_source, source_in), (leaf_inverse, linv)]
+    loads = [
+        (leaf_source, source_in),
+        (leaf_inverse, linv),
+        (strip_inverse, sinv),
+        (summit_strip, slift),
+        (coupling, link),
+        (summit_band, lift_in),
+    ]
     for a in range(1, leaves):
         part = pl.ds(pair(a, 0), a)
         loads.append((leaf_blocks.at[part], lblk.at[part]))
@@ -114,12 +129,8 @@
         (band_source, border_in.at[0]),
         (strip_source, border_in.at[1]),
         (summit_source, border_in.at[2]),
-        (coupling, link),
         (band_inverse, binv),
-        (strip_inverse, sinv),
         (summit_inverse, uinv),
-        (summit_band, lift_in),
-        (summit_strip, slift),
     ]
     copies = [
         pltpu.make_async_copy(src, dst, load_sem.at[place])
@@ -154,15 +165,17 @@
     used = []
 
     def ship(make_src, make_dst, peers, phase):
-        for peer in peers:
-            pltpu.make_async_remote_copy(
-                src_ref=make_src(peer),
-                dst_ref=make_dst(peer),
-                send_sem=send_sem.at[phase],
-                recv_sem=recv_sem.at[phase],
-                device_id=peer,
-                device_id_type=MESH,
-            ).start()
+        @pl.when(c >= 0)
+        def _():
+            for peer in peers:
+                pltpu.make_async_remote_copy(
+                    src_ref=make_src(peer),
+                    dst_ref=make_dst(peer),
+                    send_sem=send_sem.at[phase],
+                    recv_sem=recv_sem.at[phase],
+                    device_id=peer,
+                    device_id_type=MESH,
+                ).start()
 
     def scatter(axis, phase, source, land):
         dim, me, peers = axis
@@ -187,6 +200,28 @@
             device_id_type=MESH,
         )
 
+    def meet(phase, source, land):
+        pltpu.make_async_remote_copy(
+            src_ref=source,
+            dst_ref=land,
+            send_sem=send_sem.at[phase],
+            recv_sem=recv_sem.at[phase],
+            device_id=twin,
+            device_id_type=MESH,
+        ).start()
+
+    def gather(phase, source, land):
+        copy = pltpu.make_async_remote_copy(
+            src_ref=source,
+            dst_ref=land,
+            send_sem=send_sem.at[phase],
+            recv_sem=recv_sem.at[phase],
+            device_id=twin,
+            device_id_type=MESH,
+        )
+        copy.wait_recv()
+        copy.wait_send()
+
     def finish(axis, phase, land):
         bytes_of(axis[2], land, phase).wait_recv()
 
@@ -208,20 +243,35 @@
     def rounded(value):
         return value.astype(BF16).astype(F32)
 
-    def forward_step(a):
-        rest = now[a].astype(F32)
-        for b in range(a):
-            rest = rest - nt(solved[b], lblk[pair(a, b)])
-        solved[a] = nt(rest.astype(BF16), linv[a]).astype(BF16)
+    def build_bridge(i):
+        below = nn(linv[2 * i + 1], lblk[pair(2 * i + 1, 2 * i)]).astype(BF16)
+        bridge[i] = nn(below, linv[2 * i]).astype(BF16)
+
+    def forward_step(i):
+        rests = []
+        for a in (2 * i, 2 * i + 1):
+            rest = now[a].astype(F32)
+            for b in range(2 * i):
+                rest = rest - nt(solved[b], lblk[pair(a, b)])
+            rests.append(rest.astype(BF16))
+        solved[2 * i] = nt(rests[0], linv[2 * i]).astype(BF16)
+        answer = nt(rests[1], linv[2 * i + 1]) - nt(rests[0], bridge[i])
+        solved[2 * i + 1] = answer.astype(BF16)
 
     def backward_chain():
-        for a in reversed(range(leaves)):
-            rest = solved[a].astype(F32)
-            for b in range(a + 1, leaves):
-                rest = rest - nn(solved[b], lblk[pair(b, a)])
-            answer = nn(rest.astype(BF16), linv[a])
-            pend[a] = answer
-            solved[a] = answer.astype(BF16)
+        for i in reversed(range(leaves // 2)):
+            rests = []
+            for a in (2 * i, 2 * i + 1):
+                rest = solved[a].astype(F32)
+                for b in range(2 * i + 2, leaves):
+                    rest = rest - nn(solved[b], lblk[pair(b, a)])
+                rests.append(rest.astype(BF16))
+            answer = nn(rests[0], linv[2 * i]) - nn(rests[1], bridge[i])
+            pend[2 * i] = answer
+            solved[2 * i] = answer.astype(BF16)
+            answer = nn(rests[1], linv[2 * i + 1])
+            pend[2 * i + 1] = answer
+            solved[2 * i + 1] = answer.astype(BF16)
 
     def term(values, blocks, place):
         part = pl.ds(place * size, size)
@@ -230,18 +280,35 @@
             result = result + nt(values[a], blocks[a, part, :])
         return result
 
-    copies[0].wait()
-    copies[1].wait()
+    extra = 2 + 8 * PASSES
+    slab = lift_in.shape[0]
+    for copy in copies[:6]:
+        copy.wait()
     prepare(0)
-    for a in range(leaves):
-        if a + 1 < leaves:
-            copies[2 + a].wait()
-            prepare(a + 1)
-        forward_step(a)
-    for copy in copies[leaves + 1 :]:
+    copies[6].wait()
+    prepare(1)
+    build_bridge(0)
+    for i in range(leaves // 2):
+        if i + 1 < leaves // 2:
+            for a in (2 * i + 2, 2 * i + 3):
+                copies[5 + a].wait()
+                prepare(a)
+            build_bridge(i + 1)
+        forward_step(i)
+        if i == 0:
+            lift[...] = jnp.zeros_like(lift)
+            lift[pl.ds(pl.multiple_of(c * slab, slab), slab), :] = lift_in[...]
+            turned = sinv[...].astype(F32).T.astype(BF16)
+            lowered[...] = nn(turned, slift[...]).astype(BF16)
+        if i == 1:
+            turned = link[...].astype(F32).T.astype(BF16)
+            ahead = nn(turned, lowered[...]) - lift[...].astype(F32)
+            send_mat[...] = ahead.reshape(send_mat.shape)
+            pl.semaphore_wait(barrier, rows + cols - 2)
+            scatter(along_cols, extra, send_mat, land_mat.at[0])
+    for copy in copies[leaves + 5 :]:
         copy.wait()
     sends[0] = parts(term(solved, stack, 0), cols)
-    pl.semaphore_wait(barrier, rows + cols - 2)
     scatter(along_cols, 0, sends.at[0], lands.at[0])
 
     strip_term = term(solved, stack, 1)
@@ -253,45 +320,34 @@
     strip_src = slabs[1, r]
     summit_src = slabs[2, c]
     strip_now = slabs[1].reshape(count, size)
-    lift[...] = jnp.zeros_like(lift)
-    slab = lift_in.shape[0]
-    lift[pl.ds(pl.multiple_of(c * slab, slab), slab), :] = lift_in[...]
-    turned = sinv[...].astype(F32).T.astype(BF16)
-    lowered[...] = nn(turned, slift[...]).astype(BF16)
     joined[...] = nn(sinv[...], link[...]).astype(BF16)
-    turned = link[...].astype(F32).T.astype(BF16)
-    send_mats[:, 0] = (nn(turned, lowered[...]) - lift[...].astype(F32)).reshape(cols, slab, size)
-
-    def key_step(a):
-        rest = stack[a].astype(F32)
-        for b in range(a + 1, leaves):
-            rest = rest - nn(keys[b], lblk[pair(b, a)])
-        keys[a] = nn(rest.astype(BF16), linv[a]).astype(BF16)
-
-    half = leaves // 2
-    for a in reversed(range(half, leaves)):
-        key_step(a)
+
+    def key_step(i):
+        rests = []
+        for a in (2 * i, 2 * i + 1):
+            rest = stack[a].astype(F32)
+            for b in range(2 * i + 2, leaves):
+                rest = rest - nn(keys[b], lblk[pair(b, a)])
+            rests.append(rest.astype(BF16))
+        keys[2 * i] = (nn(rests[0], linv[2 * i]) - nn(rests[1], bridge[i])).astype(BF16)
+        keys[2 * i + 1] = nn(rests[1], linv[2 * i + 1]).astype(BF16)
+
+    pairs = leaves // 2
+    key_step(pairs - 1)
+    key_step(pairs - 2)
     finish(along_cols, 0, lands.at[0])
     rest = band_src - total(lands[0])
     band_slab = rounded(nt(rest.astype(BF16), binv[...]))
     spread(along_cols, 1, band_slab, lands.at[1])
-    for a in reversed(range(half)):
-        key_step(a)
-    cross = nt(keys[0, pl.ds(0, size), :], keys[0])
-    for a in range(1, leaves):
-        cross = cross + nt(keys[a, pl.ds(0, size), :], keys[a])
-    band_strip = cross[:, size : 2 * size].astype(BF16)
-    send_mats[:, 1] = cross[:, :size].reshape(cols, slab, size)
-    send_mats[:, 2] = (nn(band_strip, lowered[...]) - cross[:, 2 * size :]).reshape(
-        cols, slab, size
-    )
+    key_step(pairs - 3)
     finish(along_cols, 1, lands.at[1])
     band_all = full(lands[1])
 
-    mats = None
+    low = pl.ds(0, size)
+    upper_rows = pl.ds(size, 2 * size)
     for p in range(PASSES):
         first = p == 0
-        base = 2 + 7 * p
+        base = 2 + 8 * p
         pushed = strip_term + nt(band_all, link[...])
         sends[base] = parts(pushed, rows)
         scatter(along_rows, base, sends.at[base], lands.at[base])
@@ -302,85 +358,108 @@
         sends[base + 1] = parts(raised, cols)
         scatter(along_cols, base + 1, sends.at[base + 1], lands.at[base + 1])
         if first:
-            mat_phase = 2 + 7 * PASSES
-            scatter(along_cols, mat_phase, send_mats, land_mats.at[0])
+            finish(along_cols, extra, land_mat.at[0])
+            spread(along_cols, extra + 1, total(land_mat[0]), land_mat.at[1])
+            for i in reversed(range(pairs - 3)):
+                key_step(i)
+            cross = nt(keys[0, low, :], keys[0])
+            for a in range(1, leaves):
+                cross = cross + nt(keys[a, low, :], keys[a])
+            band_strip[...] = cross[:, size : 2 * size].astype(BF16)
+            send_mats[:, 0] = cross[:, :size].reshape(cols, slab, size)
+            product = nn(band_strip[...], lowered[...])
+            send_mats[:, 1] = (product - cross[:, 2 * size :]).reshape(cols, slab, size)
+            scatter(along_cols, extra + 2, send_mats, land_mats.at[0])
         else:
-            for a in range(leaves):
-                forward_step(a)
-        backward_chain()
+            for i in range(pairs):
+                forward_step(i)
         finish(along_rows, base, lands.at[base])
         rest = strip_src - total(lands[base])
         strip_slab = rounded(nt(rest.astype(BF16), sinv[...]))
         spread(along_rows, base + 2, strip_slab, lands.at[base + 2])
         finish(along_cols, base + 1, lands.at[base + 1])
-        spread(along_rows, base + 3, total(lands[base + 1]), lands.at[base + 3])
+        own = total(lands[base + 1])
+        land_twin[p, 0] = own
+        meet(base + 3, land_twin.at[p, 0], land_twin.at[p, 1])
+        backward_chain()
         if first:
-            finish(along_cols, mat_phase, land_mats.at[0])
-            spread(along_cols, mat_phase + 1, total(land_mats[0]), land_mats.at[1])
             next_term = term(solved, keys, 0)
+        gather(base + 3, land_twin.at[p, 0], land_twin.at[p, 1])
+        spread(along_chips, base + 4, own + land_twin[p, 1], lands.at[base + 4])
         finish(along_rows, base + 2, lands.at[base + 2])
         strip_all = full(lands[base + 2])
         dropped = nn(strip_all, joined[...])
         strip_own = nn(strip_all, sinv[...])
         if first:
             send_pair[:, 0] = parts(dropped, cols)
-            send_pair[:, 1] = parts(next_term - nt(strip_own.astype(BF16), band_strip), cols)
-            scatter(along_cols, base + 4, send_pair, land_pair.at[0])
+            next_term = next_term - nt(strip_own.astype(BF16), band_strip[...])
+            send_pair[:, 1] = parts(next_term, cols)
+            scatter(along_cols, base + 5, send_pair, land_pair.at[0])
+            finish(along_cols, extra + 2, land_mats.at[0])
+            spread(along_cols, extra + 3, total(land_mats[0]), land_mats.at[1])
+            finish(along_cols, extra + 1, land_mat.at[1])
+            ahead_all[...] = land_mat[1].reshape(size, size).astype(BF16)
         else:
-            sends[base + 4] = parts(dropped, cols)
-            scatter(along_cols, base + 4, sends.at[base + 4], lands.at[base + 4])
-        finish(along_rows, base + 3, lands.at[base + 3])
-        rest = summit_src - total(lands[base + 3])
+            sends[base + 5] = parts(dropped, cols)
+            scatter(along_cols, base + 5, sends.at[base + 5], lands.at[base + 5])
+        finish(along_chips, base + 4, lands.at[base + 4])
+        rest = summit_src - total(lands[base + 4, : rows // 2])
         top = nt(rest.astype(BF16), uinv[...]).astype(BF16)
         top = nn(top, uinv[...]).astype(BF16)
         summit_src = top.astype(F32)
-        spread(along_cols, base + 5, summit_src, lands.at[base + 5])
+        spread(along_cols, base + 6, summit_src, lands.at[base + 6])
+        back = nt(top, ahead_all[...])
         if first:
-            finish(along_cols, mat_phase + 1, land_mats.at[1])
-            mats = [land_mats[1, :, k].reshape(size, size).astype(BF16) for k in range(3)]
-            lblk_back = nt(top, mats[2])
-        back = nt(top, mats[0])
-        if first:
-            finish(along_cols, base + 4, land_pair.at[0])
+            finish(along_cols, base + 5, land_pair.at[0])
             sums = total(land_pair[0])
             rest = band_slab - sums[0] + back
-            band_answer = nn(rest.astype(BF16), binv[...]).astype(BF16)
-            rest = band_answer.astype(F32) - sums[1] + nt(band_answer, mats[1]) - lblk_back
-            band_slab = rounded(nt(rest.astype(BF16), binv[...]))
-            both = jnp.stack([band_answer.astype(F32), band_slab])
-            spread(along_cols, base + 6, both, land_pair.at[1])
+            band_answer = rounded(nn(rest.astype(BF16), binv[...]))
+            shift = nt(sums[1].astype(BF16), binv[...])
+            spread(along_cols, base + 7, jnp.stack([band_answer, shift]), land_pair.at[1])
         else:
-            finish(along_cols, base + 4, lands.at[base + 4])
-            rest = band_slab - total(lands[base + 4]) + back
+            finish(along_cols, base + 5, lands.at[base + 5])
+            rest = band_slab - total(lands[base + 5]) + back
             band_answer = rounded(nn(rest.astype(BF16), binv[...]))
-            spread(along_cols, base + 6, band_answer, lands.at[base + 6])
-        finish(along_cols, base + 5, lands.at[base + 5])
-        top_all = full(lands[base + 5])
+            spread(along_cols, base + 7, band_answer, lands.at[base + 7])
+        finish(along_cols, base + 6, lands.at[base + 6])
+        top_all = full(lands[base + 6])
         strip_answer = (strip_own - nt(top_all, lowered[...])).astype(BF16)
         strip_now = strip_answer.astype(F32)
+        upper = jnp.concatenate([strip_answer, top_all], axis=1)
+        for a in range(leaves):
+            rest = pend[a] - nn(upper, keys[a, upper_rows, :])
+            pend[a] = rest
+            if first:
+                now[a] = rest.astype(BF16)
         if first:
             slabs[1] = parts(strip_now, rows)
             strip_src = slabs[1, r]
-        upper = jnp.concatenate([strip_answer, top_all], axis=1)
-        lower_rows = pl.ds(size, 2 * size)
+            strip_term = term(now, keys, 1)
+            finish(along_cols, extra + 3, land_mats.at[1])
+            fold = land_mats[1, :, 0].reshape(size, size).astype(BF16)
+            ahead_mat = binv[...].astype(F32) + nn(binv[...], fold)
+            ahead_mat = ahead_mat.astype(BF16)
+            fold = land_mats[1, :, 1].reshape(size, size).astype(BF16)
+            lag = nn(binv[...], fold).astype(BF16)
+            lagging = nt(top_all, lag)
+            finish(along_cols, base + 7, land_pair.at[1])
+            band_full = full(land_pair[1, :, 0])
+            lagging = lagging + land_pair[1, :, 1].reshape(count, size)
+            band_next = nt(band_full, ahead_mat) - lagging
+            band_all = band_next.astype(BF16)
+            band_place = rounded(band_next).reshape(cols, count // cols, size)
+            slabs[0] = band_place
+            band_slab = slabs[0, c]
+            strip_term = strip_term - nn(band_full, band_strip[...])
+        else:
+            finish(along_cols, base + 7, lands.at[base + 7])
+            band_full = full(lands[base + 7])
         for a in range(leaves):
-            pend[a] -= nn(upper, keys[a, lower_rows, :])
-        if first:
-            finish(along_cols, base + 6, land_pair.at[1])
-            band_full = full(land_pair[1, :, 0])
-            band_all = full(land_pair[1, :, 1])
-        else:
-            finish(along_cols, base + 6, lands.at[base + 6])
-            band_full = full(lands[base + 6])
-        place = pl.ds(0, size)
-        for a in range(leaves):
-            value = (pend[a] - nn(band_full, keys[a, place, :])).astype(BF16)
+            value = (pend[a] - nn(band_full, keys[a, low, :])).astype(BF16)
             if first:
                 now[a] = value
             else:
                 leaf_out[a] = value
-        if first:
-            strip_term = term(now, keys, 1)
     border_out[0] = band_full
     border_out[1] = strip_answer
     border_out[2] = top_all
@@ -425,7 +504,7 @@
     scalars = pl.BlockSpec(memory_space=pltpu.SMEM)
     vmem = pl.BlockSpec(memory_space=pltpu.VMEM)
     plain = pltpu.VMEM(square, BF16)
-    phases = 4 + 7 * PASSES
+    phases = 6 + 8 * PASSES
     solved = pl.pallas_call(
         functools.partial(kernel, rows, cols),
         out_shape=(
@@ -439,6 +518,7 @@
             pltpu.VMEM((3, size, count), BF16),
             pltpu.VMEM((leaves,) + square, BF16),
             pltpu.VMEM((pairs,) + square, BF16),
+            pltpu.VMEM((leaves // 2,) + square, BF16),
             pltpu.VMEM((leaves, 3 * size, size), BF16),
             pltpu.VMEM((leaves, 3 * size, size), BF16),
             plain,
@@ -455,11 +535,16 @@
             pltpu.VMEM((leaves, count, size), F32),
             pltpu.VMEM((3, cols, band_rhs, size), F32),
             pltpu.VMEM((phases, cols, band_rhs, size), F32),
-            pltpu.VMEM((cols, 3, slab, size), F32),
+            pltpu.VMEM((cols, slab, size), F32),
+            pltpu.VMEM((cols, 2, slab, size), F32),
             pltpu.VMEM((cols, 2, band_rhs, size), F32),
             pltpu.VMEM((phases, cols, band_rhs, size), F32),
-            pltpu.VMEM((2, cols, 3, slab, size), F32),
+            pltpu.VMEM((2, cols, slab, size), F32),
+            pltpu.VMEM((2, cols, 2, slab, size), F32),
             pltpu.VMEM((2, cols, 2, band_rhs, size), F32),
+            pltpu.VMEM((PASSES, 2, band_rhs, size), F32),
+            plain,
+            plain,
             pltpu.SemaphoreType.DMA((32,)),
             pltpu.SemaphoreType.DMA((phases,)),
             pltpu.SemaphoreType.DMA((phases,)),

time: 82 us -> 76.7 us (0.935)
  Pallas kernels: 81.3 us -> 75.9 us
    pallas_call x1, Pallas kernels: 79.1 us -> 73.8 us  [per_device(): pl.pallas_call(functools.partial(kernel, rows, cols), out_shape=(jax.Shap...]
where the time goes in v3:
time: 76.7 us; the launch traced here: 76.6 us
  Pallas kernels  75.9 us (99%)
    pallas_call x1, Pallas kernels, per_device(): pl.pallas_call(functools.partial(kernel, rows, cols), out_shape=(jax.Shap...  73.8 us
    pallas_call x1, Pallas kernels, per_device(): pl.pallas_call(turn, out_shape=(jax.ShapeDtypeStruct((leaves, size, count...  2.14 us

profile of v3, /device:TPU:1, one launch (start us, length us, event | category | flops | bytes accessed | tf_op | source)
XLA Modules:
  0.0 76.6 jit_solution(9162284842773261824)
XLA Ops:
  0.6 73.8 %shard_map.192 = (bf16[8,128,256]{2,1,0:T(8,128)(2,1)}, bf16[3,128,256]{2,1,0:T(8,128)(2,1)}) custom-call(s32[8]{0:T(128)} %bitcast.34, s32[8]{0:T(128)} %bitcast.35, bf16[8,256,128]{2,1,0:T(8,128)(2,1)} %bitcast.23, bf16[256,128]{1,0:T(8,128)(2,1)} %bitcast.29, bf16[256,128]{1,0:T(8,128)(2,1)} %bitcast.30, bf16[256,128]{1,0:T(8,128)(2,1)} %summit_source.1, ...), custom_call_target="tpu_custom_call" | custom-call | flops 4400000000 | bytes 10000000 | tf_op jit(solution)/shard_map/pallas_call | solution.py:508
  74.5 2.1 %shard_map.193 = (bf16[8,256,128]{2,1,0:T(8,128)(2,1)}, bf16[256,128]{1,0:T(8,128)(2,1)}, bf16[256,128]{1,0:T(8,128)(2,1)}, bf16[256,128]{1,0:T(8,128)(2,1)}) custom-call(bf16[8,128,256]{2,1,0:T(8,128)(2,1)} %get-tuple-element.10.leaf_in, bf16[3,128,256]{2,1,0:T(8,128)(2,1)} %get-tuple-element.11.border_in), custom_call_target="tpu_custom_call" | custom-call | tf_op jit(solution)/shard_map/pallas_call | solution.py:577

commit v4 on v3

--- a/solution.py
+++ b/solution.py
@@ -64,6 +64,7 @@
     lowered,
     joined,
     now,
+    upright,
     solved,
     pend,
     slabs,
@@ -114,16 +115,16 @@
     loads = [
         (leaf_source, source_in),
         (leaf_inverse, linv),
-        (strip_inverse, sinv),
-        (summit_strip, slift),
-        (coupling, link),
-        (summit_band, lift_in),
     ]
     for a in range(1, leaves):
         part = pl.ds(pair(a, 0), a)
         loads.append((leaf_blocks.at[part], lblk.at[part]))
     loads += [
         (band_blocks, whole(0)),
+        (strip_inverse, sinv),
+        (summit_strip, slift),
+        (coupling, link),
+        (summit_band, lift_in),
         (strip_blocks, whole(1)),
         (summit_blocks, whole(2)),
         (band_source, border_in.at[0]),
@@ -136,7 +137,8 @@
         pltpu.make_async_copy(src, dst, load_sem.at[place])
         for place, (src, dst) in enumerate(loads)
     ]
-    for copy in copies:
+    soon = leaves + 2
+    for copy in copies[:soon]:
         copy.start()
 
     barrier = pltpu.get_barrier_semaphore()
@@ -157,7 +159,6 @@
 
     def prepare(a):
         linv[a] = jnp.where(furthest < widths[a], linv[a].astype(F32), 0.0).astype(BF16)
-        now[a] = source_in[a].astype(F32).T.astype(BF16)
         for b in range(a):
             weight = reach[a, b].astype(F32)
             lblk[pair(a, b)] = (lblk[pair(a, b)].astype(F32) * weight).astype(BF16)
@@ -257,6 +258,17 @@
         solved[2 * i] = nt(rests[0], linv[2 * i]).astype(BF16)
         answer = nt(rests[1], linv[2 * i + 1]) - nt(rests[0], bridge[i])
         solved[2 * i + 1] = answer.astype(BF16)
+
+    def first_step(i):
+        rests = []
+        for a in (2 * i, 2 * i + 1):
+            rest = source_in[a].astype(F32)
+            for b in range(2 * i):
+                rest = rest - nn(lblk[pair(a, b)], upright[b])
+            rests.append(rest.astype(BF16))
+        upright[2 * i] = nn(linv[2 * i], rests[0]).astype(BF16)
+        answer = nn(linv[2 * i + 1], rests[1]) - nn(bridge[i], rests[0])
+        upright[2 * i + 1] = answer.astype(BF16)
 
     def backward_chain():
         for i in reversed(range(leaves // 2)):
@@ -282,35 +294,41 @@
 
     extra = 2 + 8 * PASSES
     slab = lift_in.shape[0]
-    for copy in copies[:6]:
+    for copy in copies[:2]:
         copy.wait()
     prepare(0)
-    copies[6].wait()
+    copies[2].wait()
     prepare(1)
     build_bridge(0)
     for i in range(leaves // 2):
         if i + 1 < leaves // 2:
             for a in (2 * i + 2, 2 * i + 3):
-                copies[5 + a].wait()
+                copies[1 + a].wait()
                 prepare(a)
             build_bridge(i + 1)
-        forward_step(i)
-        if i == 0:
-            lift[...] = jnp.zeros_like(lift)
-            lift[pl.ds(pl.multiple_of(c * slab, slab), slab), :] = lift_in[...]
-            turned = sinv[...].astype(F32).T.astype(BF16)
-            lowered[...] = nn(turned, slift[...]).astype(BF16)
-        if i == 1:
-            turned = link[...].astype(F32).T.astype(BF16)
-            ahead = nn(turned, lowered[...]) - lift[...].astype(F32)
-            send_mat[...] = ahead.reshape(send_mat.shape)
-            pl.semaphore_wait(barrier, rows + cols - 2)
-            scatter(along_cols, extra, send_mat, land_mat.at[0])
-    for copy in copies[leaves + 5 :]:
+        first_step(i)
+        if i == leaves // 2 - 2:
+            for copy in copies[soon:]:
+                copy.start()
+    copies[soon - 1].wait()
+    start_term = nn(stack[0, pl.ds(0, size), :], upright[0])
+    for a in range(1, leaves):
+        start_term = start_term + nn(stack[a, pl.ds(0, size), :], upright[a])
+    sends[0] = parts(start_term.T, cols)
+    pl.semaphore_wait(barrier, rows + cols - 2)
+    scatter(along_cols, 0, sends.at[0], lands.at[0])
+    for copy in copies[soon:]:
         copy.wait()
-    sends[0] = parts(term(solved, stack, 0), cols)
-    scatter(along_cols, 0, sends.at[0], lands.at[0])
-
+    lift[...] = jnp.zeros_like(lift)
+    lift[pl.ds(pl.multiple_of(c * slab, slab), slab), :] = lift_in[...]
+    turned = sinv[...].astype(F32).T.astype(BF16)
+    lowered[...] = nn(turned, slift[...]).astype(BF16)
+    turned = link[...].astype(F32).T.astype(BF16)
+    ahead = nn(turned, lowered[...]) - lift[...].astype(F32)
+    send_mat[...] = ahead.reshape(send_mat.shape)
+
+    for a in range(leaves):
+        solved[a] = upright[a].astype(F32).T.astype(BF16)
     strip_term = term(solved, stack, 1)
     summit_term = term(solved, stack, 2)
     slabs[0] = parts(border_in[0].astype(F32).T, cols)
@@ -339,7 +357,9 @@
     rest = band_src - total(lands[0])
     band_slab = rounded(nt(rest.astype(BF16), binv[...]))
     spread(along_cols, 1, band_slab, lands.at[1])
-    key_step(pairs - 3)
+    scatter(along_cols, extra, send_mat, land_mat.at[0])
+    for i in reversed(range(pairs - 2)):
+        key_step(i)
     finish(along_cols, 1, lands.at[1])
     band_all = full(lands[1])
 
@@ -360,8 +380,6 @@
         if first:
             finish(along_cols, extra, land_mat.at[0])
             spread(along_cols, extra + 1, total(land_mat[0]), land_mat.at[1])
-            for i in reversed(range(pairs - 3)):
-                key_step(i)
             cross = nt(keys[0, low, :], keys[0])
             for a in range(1, leaves):
                 cross = cross + nt(keys[a, low, :], keys[a])
@@ -531,6 +549,7 @@
             plain,
             plain,
             pltpu.VMEM((leaves, count, size), BF16),
+            pltpu.VMEM((leaves, size, count), BF16),
             pltpu.VMEM((leaves, count, size), BF16),
             pltpu.VMEM((leaves, count, size), F32),
             pltpu.VMEM((3, cols, band_rhs, size), F32),

time: 76.7 us -> 75.6 us (0.986)
  Pallas kernels: 75.9 us -> 74.8 us
    pallas_call x1, Pallas kernels: 73.8 us -> 72.6 us  [per_device(): pl.pallas_call(functools.partial(kernel, rows, cols), out_shape=(jax.Shap...]
where the time goes in v4:
time: 75.6 us; the launch traced here: 75.4 us
  Pallas kernels  74.8 us (99%)
    pallas_call x1, Pallas kernels, per_device(): pl.pallas_call(functools.partial(kernel, rows, cols), out_shape=(jax.Shap...  72.6 us
    pallas_call x1, Pallas kernels, per_device(): pl.pallas_call(turn, out_shape=(jax.ShapeDtypeStruct((leaves, size, count...  2.14 us

profile of v4, /device:TPU:1, one launch (start us, length us, event | category | flops | bytes accessed | tf_op | source)
XLA Modules:
  0.0 75.4 jit_solution(3767926969118117144)
XLA Ops:
  0.6 72.6 %shard_map.192 = (bf16[8,128,256]{2,1,0:T(8,128)(2,1)}, bf16[3,128,256]{2,1,0:T(8,128)(2,1)}) custom-call(s32[8]{0:T(128)} %bitcast.34, s32[8]{0:T(128)} %bitcast.35, bf16[8,256,128]{2,1,0:T(8,128)(2,1)} %bitcast.23, bf16[256,128]{1,0:T(8,128)(2,1)} %bitcast.29, bf16[256,128]{1,0:T(8,128)(2,1)} %bitcast.30, bf16[256,128]{1,0:T(8,128)(2,1)} %summit_source.1, ...), custom_call_target="tpu_custom_call" | custom-call | flops 4400000000 | bytes 10000000 | tf_op jit(solution)/shard_map/pallas_call | solution.py:526
  73.3 2.1 %shard_map.193 = (bf16[8,256,128]{2,1,0:T(8,128)(2,1)}, bf16[256,128]{1,0:T(8,128)(2,1)}, bf16[256,128]{1,0:T(8,128)(2,1)}, bf16[256,128]{1,0:T(8,128)(2,1)}) custom-call(bf16[8,128,256]{2,1,0:T(8,128)(2,1)} %get-tuple-element.10.leaf_in, bf16[3,128,256]{2,1,0:T(8,128)(2,1)} %get-tuple-element.11.border_in), custom_call_target="tpu_custom_call" | custom-call | tf_op jit(solution)/shard_map/pallas_call | solution.py:596

commit v5 on v4

--- a/solution.py
+++ b/solution.py
@@ -353,17 +353,25 @@
     pairs = leaves // 2
     key_step(pairs - 1)
     key_step(pairs - 2)
+    key_step(pairs - 3)
     finish(along_cols, 0, lands.at[0])
     rest = band_src - total(lands[0])
     band_slab = rounded(nt(rest.astype(BF16), binv[...]))
     spread(along_cols, 1, band_slab, lands.at[1])
     scatter(along_cols, extra, send_mat, land_mat.at[0])
-    for i in reversed(range(pairs - 2)):
+    for i in reversed(range(pairs - 3)):
         key_step(i)
+    low = pl.ds(0, size)
+    cross = nt(keys[0, low, :], keys[0])
+    for a in range(1, leaves):
+        cross = cross + nt(keys[a, low, :], keys[a])
+    band_strip[...] = cross[:, size : 2 * size].astype(BF16)
+    send_mats[:, 0] = cross[:, :size].reshape(cols, slab, size)
+    product = nn(band_strip[...], lowered[...])
+    send_mats[:, 1] = (product - cross[:, 2 * size :]).reshape(cols, slab, size)
     finish(along_cols, 1, lands.at[1])
     band_all = full(lands[1])
 
-    low = pl.ds(0, size)
     upper_rows = pl.ds(size, 2 * size)
     for p in range(PASSES):
         first = p == 0
@@ -378,16 +386,9 @@
         sends[base + 1] = parts(raised, cols)
         scatter(along_cols, base + 1, sends.at[base + 1], lands.at[base + 1])
         if first:
+            scatter(along_cols, extra + 2, send_mats, land_mats.at[0])
             finish(along_cols, extra, land_mat.at[0])
             spread(along_cols, extra + 1, total(land_mat[0]), land_mat.at[1])
-            cross = nt(keys[0, low, :], keys[0])
-            for a in range(1, leaves):
-                cross = cross + nt(keys[a, low, :], keys[a])
-            band_strip[...] = cross[:, size : 2 * size].astype(BF16)
-            send_mats[:, 0] = cross[:, :size].reshape(cols, slab, size)
-            product = nn(band_strip[...], lowered[...])
-            send_mats[:, 1] = (product - cross[:, 2 * size :]).reshape(cols, slab, size)
-            scatter(along_cols, extra + 2, send_mats, land_mats.at[0])
         else:
             for i in range(pairs):
                 forward_step(i)

time: 75.6 us -> 76.1 us (level)
  no operation moved by 1% of the time
where the time goes in v5:
time: 76.1 us; the launch traced here: 76 us
  Pallas kernels  75.3 us (99%)
    pallas_call x1, Pallas kernels, per_device(): pl.pallas_call(functools.partial(kernel, rows, cols), out_shape=(jax.Shap...  73.2 us
    pallas_call x1, Pallas kernels, per_device(): pl.pallas_call(turn, out_shape=(jax.ShapeDtypeStruct((leaves, size, count...  2.14 us

profile of v5, /device:TPU:1, one launch (start us, length us, event | category | flops | bytes accessed | tf_op | source)
XLA Modules:
  0.0 76.0 jit_solution(3952576192704657732)
XLA Ops:
  0.6 73.2 %shard_map.192 = (bf16[8,128,256]{2,1,0:T(8,128)(2,1)}, bf16[3,128,256]{2,1,0:T(8,128)(2,1)}) custom-call(s32[8]{0:T(128)} %bitcast.34, s32[8]{0:T(128)} %bitcast.35, bf16[8,256,128]{2,1,0:T(8,128)(2,1)} %bitcast.23, bf16[256,128]{1,0:T(8,128)(2,1)} %bitcast.29, bf16[256,128]{1,0:T(8,128)(2,1)} %bitcast.30, bf16[256,128]{1,0:T(8,128)(2,1)} %summit_source.1, ...), custom_call_target="tpu_custom_call" | custom-call | flops 4400000000 | bytes 10000000 | tf_op jit(solution)/shard_map/pallas_call | solution.py:527
  73.8 2.1 %shard_map.193 = (bf16[8,256,128]{2,1,0:T(8,128)(2,1)}, bf16[256,128]{1,0:T(8,128)(2,1)}, bf16[256,128]{1,0:T(8,128)(2,1)}, bf16[256,128]{1,0:T(8,128)(2,1)}) custom-call(bf16[8,128,256]{2,1,0:T(8,128)(2,1)} %get-tuple-element.10.leaf_in, bf16[3,128,256]{2,1,0:T(8,128)(2,1)} %get-tuple-element.11.border_in), custom_call_target="tpu_custom_call" | custom-call | tf_op jit(solution)/shard_map/pallas_call | solution.py:597
